TPU v7x, 32 devices: a whole 2x2x4 slice. The times are simulated.
32 devices in a mesh: shard: 2 (over core), context: 4 (over y, x), tensor: 4 (over z).
Axes of the slice: x: 2, y: 2, z: 4, core: 2. Of those that a mesh axis runs over, the one named last changes fastest.
Arguments:
- tokens: bfloat16 [2, 4, 256, 2048], P('shard', 'context', None, 'tensor'), may hold values from -6 to 6
- parents: int32 [2, 4], P('shard'), may hold values from -1 to 3, as said below
- routes: int32 [2, 4, 256, 8], P('shard', 'context'), may hold values from 0 to 63, all different within a row
- pair_order: int32 [2, 4, 2048], P('shard', 'context'), may hold values from 0 to 2047, each once within a row
- norm_attn: bfloat16 [2048], P(('shard', 'context')), may hold values from 0.5 to 1.5
- w_query: bfloat16 [2048, 2048], P(('shard', 'context'), 'tensor'), may hold values from -0.125 to 0.125
- w_key: bfloat16 [2048, 2048], P(('shard', 'context'), 'tensor'), may hold values from -0.125 to 0.125
- w_value: bfloat16 [2048, 2048], P(('shard', 'context'), 'tensor'), may hold values from -0.125 to 0.125
- q_gain: bfloat16 [16, 128], P('tensor', ('shard', 'context')), may hold values from 0.099609375 to 1.8984375
- k_gain: bfloat16 [16, 128], P('tensor', ('shard', 'context')), may hold values from 0.099609375 to 1.8984375
- w_out: bfloat16 [2048, 2048], P('tensor', ('shard', 'context')), may hold values from -1 to 1
- norm_moe: bfloat16 [2048], P(('shard', 'context')), may hold values from 0.5 to 1.5
- w_router: bfloat16 [2048, 64], P(('shard', 'context')), may hold values from -0.06591797 to 0.06591797
- w_gate: bfloat16 [64, 2048, 1024], P(('shard', 'context'), None, 'tensor'), may hold values from -0.125 to 0.125
- w_up: bfloat16 [64, 2048, 1024], P(('shard', 'context'), None, 'tensor'), may hold values from -0.125 to 0.125
- w_down: bfloat16 [64, 1024, 2048], P(('shard', 'context'), 'tensor'), may hold values from -4.5 to 4.5
- out_grad: bfloat16 [2, 4, 256, 2048], P('shard', 'context', None, 'tensor'), may hold values from -6 to 6
Outputs:
- mixed: bfloat16 [2, 4, 256, 2048], P('shard', 'context', None, 'tensor')
- tokens_grad: float32 [2, 4, 256, 2048], P('shard', 'context', None, 'tensor')
- norm_attn_grad: float32 [2048], P(('shard', 'context'))
- w_query_grad: float32 [2048, 2048], P(('shard', 'context'), 'tensor')
- w_key_grad: float32 [2048, 2048], P(('shard', 'context'), 'tensor')
- w_value_grad: float32 [2048, 2048], P(('shard', 'context'), 'tensor')
- q_gain_grad: float32 [16, 128], P('tensor', ('shard', 'context'))
- k_gain_grad: float32 [16, 128], P('tensor', ('shard', 'context'))
- w_out_grad: float32 [2048, 2048], P('tensor', ('shard', 'context'))
- norm_moe_grad: float32 [2048], P(('shard', 'context'))
- w_router_grad: float32 [2048, 64], P(('shard', 'context'))
- w_gate_grad: float32 [64, 2048, 1024], P(('shard', 'context'), None, 'tensor')
- w_up_grad: float32 [64, 2048, 1024], P(('shard', 'context'), None, 'tensor')
- w_down_grad: float32 [64, 1024, 2048], P(('shard', 'context'), 'tensor')
Inputs may be any that keep to these rules, and one draw needn't show every extreme that they name: Each row is one tree over the 4 slots with a single root (-1); following parents from any slot reaches the root. `routes`: each token names 8 different experts. `pair_order`: each segment's row is a permutation of its pairs, listed token by token, choice by choice.
All inputs are finite; a program needn't handle non-finite values.
Results may differ from a plain program's by a relative error of at most 0.017.
Values may be sent and summed in bfloat16 or wider, within the bound.
No kernel may reach another device: no remote copies, remote signals or barrier semaphores. Data moves between devices by JAX's collectives and lax.ppermute only.
A program may use at most 320 MiB of HBM per device.

v0:
```python
import jax
import jax.numpy as jnp
from jax import lax
from jax.sharding import PartitionSpec as P

EPS = 1e-05
ROPE_BASE = 10000.0
NEG_FILL = -1e30
SH, CT, TS = "shard", "context", "tensor"
F32, BF16 = jnp.float32, jnp.bfloat16


def swap(value, axis, rel):
    count = lax.axis_size(axis)
    return lax.ppermute(value, axis, [(i, i ^ rel) for i in range(count)])


def around(value, axis):
    return [value] + [swap(value, axis, rel) for rel in range(1, lax.axis_size(axis))]


def gather_groups(value):
    blocks = around(value, CT)
    for rel in range(1, lax.axis_size(SH)):
        blocks = blocks + [swap(block, SH, rel) for block in blocks[: lax.axis_size(CT)]]
    return blocks


def in_order(blocks, index):
    ordered = []
    for place in range(len(blocks)):
        picked = blocks[place]
        for mine in range(1, len(blocks)):
            picked = jnp.where(index == mine, blocks[place ^ mine], picked)
        ordered.append(picked)
    return ordered


def gather_tensor(value, axis=1):
    return jnp.concatenate(in_order(around(value, TS), lax.axis_index(TS)), axis)


def place_rows(blocks, index):
    rows = blocks[0].shape[0]
    whole = jnp.zeros((rows * len(blocks),) + blocks[0].shape[1:], blocks[0].dtype)
    for rel, block in enumerate(blocks):
        whole = lax.dynamic_update_slice_in_dim(whole, block, (index ^ rel) * rows, 0)
    return whole


def stack_blocks(blocks):
    whole = jnp.zeros((len(blocks),) + blocks[0].shape, blocks[0].dtype)
    for rel, block in enumerate(blocks):
        whole = lax.dynamic_update_index_in_dim(whole, block, rel, 0)
    return whole


def low(value):
    return value.astype(BF16)


def wide(value):
    return value.astype(F32)


def dot(left, right, left_dim=1, right_dim=0):
    return lax.dot_general(
        left, right, (((left_dim,), (right_dim,)), ((), ())), preferred_element_type=F32
    )


def group_sum(stacked):
    context_count = lax.axis_size(CT)
    mine = stacked[:context_count]
    for rel in range(1, lax.axis_size(SH)):
        other = swap(stacked[rel * context_count : (rel + 1) * context_count], SH, rel)
        mine = (wide(mine) + wide(other)).astype(stacked.dtype)
    total = wide(mine[0])
    for rel in range(1, context_count):
        total = total + wide(swap(mine[rel], CT, rel))
    return total


def group_trade(stacked):
    shard_count, context_count = lax.axis_size(SH), lax.axis_size(CT)
    parts = [stacked[:context_count]]
    for rel in range(1, shard_count):
        parts.append(swap(stacked[rel * context_count : (rel + 1) * context_count], SH, rel))
    parts = jnp.stack(parts)
    by_context = [parts[:, 0]] + [swap(parts[:, rel], CT, rel) for rel in range(1, context_count)]
    return [by_context[c][s] for s in range(shard_count) for c in range(context_count)]


def tree_info(parent_row):
    slot_count = parent_row.shape[0]
    slot_ids = jnp.arange(slot_count, dtype=jnp.int32)
    reach = (parent_row[:, None] == slot_ids[None, :]) | (slot_ids[:, None] == slot_ids[None, :])
    span = 1
    while span < slot_count:
        reach = jnp.any(reach[:, :, None] & reach[None, :, :], 1)
        span *= 2
    depths = jnp.sum(reach.astype(jnp.int32), 1) - 1
    return (reach, depths)


def rope_tables(positions, head_dim):
    half_dim = head_dim // 2
    frequency = ROPE_BASE ** (-2.0 * jnp.arange(half_dim, dtype=F32) / head_dim)
    angles = positions.astype(F32)[:, None] * frequency[None, :]
    cosine = jnp.concatenate([jnp.cos(angles), jnp.cos(angles)], -1)
    sine_table = jnp.concatenate([jnp.sin(angles), jnp.sin(angles)], -1)
    return (cosine, sine_table)


def rotate(values, cosine, sine_table):
    half_dim = values.shape[-1] // 2
    turned = jnp.concatenate([-values[..., half_dim:], values[..., :half_dim]], -1)
    return values * cosine[:, None, :] + turned * sine_table[:, None, :]


def rms_scale(values):
    return lax.rsqrt(jnp.mean(values * values, -1, keepdims=True) + EPS)


def own_slots(codes, pair_count, first_expert, expert_dev, capacity):
    expert_ids = first_expert + jnp.arange(expert_dev, dtype=jnp.int32)
    hit = (codes // pair_count)[:, :, :, None] == expert_ids
    rank = jnp.sum(jnp.where(hit, (codes % pair_count)[:, :, :, None], 0), 2)
    routed = jnp.any(hit, 2)
    rank = jnp.where(routed, rank, pair_count).transpose(0, 2, 1)
    routed = routed.transpose(0, 2, 1)
    place = jnp.sum((rank[:, :, None, :] < rank[:, :, :, None]).astype(jnp.int32), -1)
    return jnp.where(routed & (place < capacity), place, -1)


def split_low(value):
    high = low(value)
    return [high, low(value - wide(high))]


def per_device(
    tokens,
    parents,
    routes,
    pair_order,
    norm_attn,
    w_query,
    w_key,
    w_value,
    q_gain,
    k_gain,
    w_out,
    norm_moe,
    w_router,
    w_gate,
    w_up,
    w_down,
    out_grad,
):
    shard_index, context_index, tensor_index = (lax.axis_index(a) for a in (SH, CT, TS))
    context_count, tensor_count = lax.axis_size(CT), lax.axis_size(TS)
    group_count = lax.axis_size(SH) * context_count
    group = shard_index * context_count + context_index
    seg_dev, seg_len, quarter = tokens.shape[1:]
    rows = seg_dev * seg_len
    model_width = quarter * tensor_count
    slice_width = norm_attn.shape[0]
    top_count = routes.shape[3]
    expert_count = w_router.shape[1]
    expert_dev = w_gate.shape[0]
    local_heads, head_dim = q_gain.shape[0], q_gain.shape[1] * group_count
    head_width = local_heads * head_dim
    capacity = tensor_count * (
        (5 * rows * top_count + 4 * expert_count * tensor_count - 1)
        // (4 * expert_count * tensor_count)
    )
    score_scale = head_dim ** (-0.5)

    gain_size = q_gain.size
    gain_rows = jnp.concatenate([q_gain.reshape(-1), k_gain.reshape(-1)])
    gain_rows = jnp.pad(gain_rows, (0, slice_width - 2 * gain_size))
    small = jnp.concatenate(
        [w_router, norm_attn[:, None], norm_moe[:, None], gain_rows[:, None]], 1
    )
    small = jnp.pad(small, ((0, 0), (0, 128 - small.shape[1])))
    packed = jnp.concatenate([w_query, w_key, w_value, small], 1)
    packed = place_rows(gather_groups(packed), group)
    qkv_weight = packed[:, : 3 * head_width]
    small = packed[:, 3 * head_width :]
    router_weight = small[:, :expert_count]
    gain_attn = wide(small[:, expert_count])
    gain_moe = wide(small[:, expert_count + 1])
    gains = small[:, expert_count + 2].reshape(group_count, slice_width)[:, : 2 * gain_size]
    gains = gains.reshape(group_count, 2, local_heads, -1).transpose(1, 2, 0, 3)
    gain_query_row, gain_key_row = wide(gains.reshape(2, head_width))

    codes = routes.reshape(rows, top_count) * (rows * top_count) + (
        jnp.arange(seg_dev, dtype=jnp.int32)[:, None] * (seg_len * top_count) + pair_order[0]
    ).reshape(rows, top_count)
    codes = jnp.stack(gather_groups(codes))
    slots = own_slots(codes, rows * top_count, group * expert_dev, expert_dev, capacity)
    choose = low(slots[:, :, None, :] == jnp.arange(capacity, dtype=jnp.int32)[:, None])
    choose = choose.reshape(group_count, expert_dev * capacity, rows)

    hidden_in = wide(gather_tensor(tokens.reshape(rows, quarter)))
    out_weight = place_rows(gather_groups(w_out.T), group)
    grad_output = gather_tensor(out_grad.reshape(rows, quarter))
    grad_blocks = stack_blocks(gather_groups(grad_output))

    reachable, depths = tree_info(parents[0])
    first_slot = context_index * seg_dev
    local_depth = lax.dynamic_slice_in_dim(depths, first_slot, seg_dev, 0)
    offsets = jnp.arange(seg_len, dtype=jnp.int32)
    positions = (local_depth[:, None] * seg_len + offsets[None, :]).reshape(rows)
    cosine, sine_table = rope_tables(positions, head_dim)
    reach_local = lax.dynamic_slice_in_dim(reachable, first_slot, seg_dev, 0)
    masks = []
    for rel in range(context_count):
        other_slot = (context_index ^ rel) * seg_dev
        seen = lax.dynamic_slice_in_dim(reach_local, other_slot, seg_dev, 1)
        seen = seen[:, None, :, None]
        if rel == 0:
            same = jnp.eye(seg_dev, dtype=bool)[:, None, :, None]
            seen = seen & (~same | (offsets[None, :] <= offsets[:, None])[None, :, None, :])
        masks.append(jnp.broadcast_to(seen, (seg_dev, seg_len, seg_dev, seg_len)).reshape(rows, rows))
    key_mask = jnp.concatenate(masks, 1)

    scale_attn = rms_scale(hidden_in)
    normed = hidden_in * scale_attn
    attn_in = low(normed * gain_attn)
    attn_slices = group_trade(
        jnp.stack(
            [
                lax.dynamic_slice_in_dim(attn_in, (group ^ rel) * slice_width, slice_width, 1)
                for rel in range(group_count)
            ]
        )
    )
    projected = dot(attn_in, qkv_weight)
    queries = projected[:, :head_width]
    key_proj = projected[:, head_width : 2 * head_width]
    value_low = low(projected[:, 2 * head_width :])
    squares = jnp.stack([jnp.sum(queries * queries, -1), jnp.sum(key_proj * key_proj, -1)])
    squares = sum(in_order(around(squares, TS), tensor_index))
    scales = lax.rsqrt(squares / model_width + EPS)[:, :, None]
    query_hat = queries * scales[0]
    key_hat = key_proj * scales[1]

    def turn(hat, gain):
        return low(rotate((hat * gain).reshape(rows, local_heads, head_dim), cosine, sine_table))

    query_heads = turn(query_hat, gain_query_row).transpose(1, 0, 2)
    key_rot = turn(key_hat, gain_key_row).reshape(rows, head_width)
    key_value = jnp.concatenate([key_rot, value_low], 1)
    key_value = jnp.concatenate(around(key_value, CT), 0)
    key_value = key_value.reshape(context_count * rows, 2, local_heads, head_dim)
    key_heads, value_heads = key_value.transpose(1, 2, 0, 3)

    def attend(operands):
        query_one, key_one, value_one = operands
        scores = dot(query_one, key_one, 1, 1) * score_scale
        scores = jnp.where(key_mask, scores, NEG_FILL)
        row_peak = jnp.max(scores, -1, keepdims=True)
        weights = jnp.exp(scores - row_peak)
        row_total = jnp.sum(weights, -1, keepdims=True)
        return (dot(low(weights / row_total), value_one), row_peak[:, 0] + jnp.log(row_total[:, 0]))

    attended, log_total = lax.map(attend, (query_heads, key_heads, value_heads))
    attended_low = low(attended.transpose(1, 0, 2).reshape(rows, head_width))
    attended_blocks = jnp.concatenate(gather_groups(attended_low), 0)

    def tensor_parts(value):
        return [
            lax.dynamic_slice_in_dim(value, (tensor_index ^ rel) * quarter, quarter, 1)
            for rel in range(tensor_count)
        ]

    def tensor_sum(parts):
        total = wide(parts[0])
        for rel in range(1, tensor_count):
            total = total + wide(swap(low(parts[rel]), TS, rel))
        return total

    attn_share = tensor_sum(tensor_parts(dot(attended_low, out_weight, 1, 1)))
    residual_share = wide(tokens.reshape(rows, quarter)) + attn_share
    residual = wide(gather_tensor(low(residual_share)))
    scale_moe = rms_scale(residual)
    normed_moe = residual * scale_moe
    moe_in = low(normed_moe * gain_moe)
    logits = dot(moe_in, router_weight)
    exponent = jnp.exp(logits - jnp.max(logits, -1, keepdims=True))
    router_probs = exponent / jnp.sum(exponent, -1, keepdims=True)

    sent = jnp.concatenate([moe_in] + split_low(router_probs), 1)
    blocks = stack_blocks(gather_groups(sent))
    batched = (((2,), (1,)), ((0,), (0,)))
    pair_shape = (group_count, expert_dev, capacity, -1)
    picked = low(lax.dot_general(choose, blocks, batched, preferred_element_type=F32))
    picked = picked.reshape(pair_shape)
    grad_rows = low(lax.dot_general(choose, grad_blocks, batched, preferred_element_type=F32))
    grad_rows = grad_rows.reshape(pair_shape)
    pair_rows = picked[..., :model_width]
    pair_probs = wide(picked[..., model_width:]).reshape(
        group_count, expert_dev, capacity, 2, expert_count
    )
    own_expert = (
        jnp.arange(expert_count, dtype=jnp.int32)[None, :]
        == (group * expert_dev + jnp.arange(expert_dev, dtype=jnp.int32))[:, None]
    )
    pair_gates = jnp.sum(
        jnp.where(own_expert[None, :, None, :], jnp.sum(pair_probs, 3), 0.0), -1, keepdims=True
    )

    def by_expert(left, right, spec):
        return jnp.einsum(spec, left, right, preferred_element_type=F32)

    into, onto = "gekd,edf->gekf", "gekf,edf->gekd"
    gate_proj = by_expert(pair_rows, w_gate, into)
    up_proj = by_expert(pair_rows, w_up, into)
    sigmoid_gate = jax.nn.sigmoid(gate_proj)
    silu_gate = gate_proj * sigmoid_gate
    activated = low(silu_gate * up_proj)
    act_raw = by_expert(grad_rows, w_down, "gekd,efd->gekf")
    pair_dots = jnp.sum(wide(activated) * act_raw, -1, keepdims=True)
    act_grad = act_raw * pair_gates
    gate_low = low(act_grad * up_proj * sigmoid_gate * (1.0 + gate_proj * (1.0 - sigmoid_gate)))
    up_low = low(act_grad * silu_gate)
    row_grads = low(by_expert(gate_low, w_gate, onto) + by_expert(up_low, w_up, onto))
    dots = jnp.where(own_expert[None, :, None, :], pair_dots, 0.0)
    returned = jnp.concatenate([row_grads] + split_low(dots), -1)
    returned = returned.reshape(group_count, expert_dev * capacity, -1)
    combine = (((1,), (1,)), ((0,), (0,)))
    row_partial = low(lax.dot_general(choose, returned, combine, preferred_element_type=F32))
    row_total = group_sum(row_partial)

    after_rows = row_total[0, 0] * 0.0
    act_gated = low(wide(activated) * pair_gates + after_rows)
    expert_out = low(by_expert(act_gated, w_down, "gekf,efd->gekd"))
    expert_out = expert_out.reshape(group_count, expert_dev * capacity, model_width)
    mixed_partial = low(lax.dot_general(choose, expert_out, combine, preferred_element_type=F32))
    mixed_share = tensor_sum(tensor_parts(group_sum(mixed_partial)))
    mixed_out = low(residual_share + mixed_share).reshape(tokens.shape)
    down_grad = by_expert(act_gated, grad_rows, "gekf,gekd->efd")
    gate_w_grad = by_expert(pair_rows, gate_low, "gekd,gekf->edf")
    up_w_grad = by_expert(pair_rows, up_low, "gekd,gekf->edf")

    row_low = low(row_total)
    parts = [
        jnp.concatenate([part, row_low[:, model_width:]], 1)
        for part in tensor_parts(row_low[:, :model_width])
    ]
    parts = [parts[0]] + [swap(parts[rel], TS, rel) for rel in range(1, tensor_count)]
    row_share = sum(wide(part[:, :quarter]) for part in parts)
    prob_grads = sum(wide(part[:, quarter:]) for part in in_order(parts, tensor_index))
    prob_grads = prob_grads[:, :expert_count] + prob_grads[:, expert_count:]
    logit_low = low(
        router_probs * (prob_grads - jnp.sum(prob_grads * router_probs, -1, keepdims=True))
    )
    logit_blocks = gather_groups(logit_low)
    router_share = lax.dynamic_slice_in_dim(router_weight, tensor_index * quarter, quarter, 0)
    moe_in_grad = wide(gather_tensor(low(row_share + dot(logit_low, router_share, 1, 1))))
    blocks_slice = lax.dynamic_slice_in_dim(blocks, group * slice_width, slice_width, 2)
    router_grad = dot(
        blocks_slice.reshape(group_count * rows, slice_width), jnp.concatenate(logit_blocks, 0), 0, 0
    )
    gain_moe_grad = jnp.sum(moe_in_grad * normed_moe, 0)
    normed_grad = moe_in_grad * gain_moe
    residual_grad = wide(grad_output) + scale_moe * (
        normed_grad - normed_moe * jnp.mean(normed_grad * normed_moe, -1, keepdims=True)
    )
    residual_low = low(residual_grad)

    residual_slices = group_trade(
        jnp.stack(
            [
                lax.dynamic_slice_in_dim(residual_low, (group ^ rel) * slice_width, slice_width, 1)
                for rel in range(group_count)
            ]
        )
    )
    out_w_grad = dot(attended_blocks, jnp.concatenate(residual_slices, 0), 0, 0)
    grad_heads = low(dot(residual_low, out_weight))
    grad_heads = grad_heads.reshape(rows, local_heads, head_dim).transpose(1, 0, 2)

    def attend_back(operands):
        query_one, key_one, value_one, grad_one, total_one = operands
        scores = dot(query_one, key_one, 1, 1) * score_scale
        scores = jnp.where(key_mask, scores, NEG_FILL)
        probabilities = jnp.exp(scores - total_one[:, None])
        prob_grad = dot(grad_one, value_one, 1, 1)
        value_grad = dot(low(probabilities), grad_one, 0, 0)
        score_grad = probabilities * (
            prob_grad - jnp.sum(probabilities * prob_grad, -1, keepdims=True)
        )
        score_low = low(score_grad * score_scale)
        return (dot(score_low, key_one), low(dot(score_low, query_one, 0, 0)), low(value_grad))

    query_grad, key_grad, value_grad = lax.map(
        attend_back, (query_heads, key_heads, value_heads, grad_heads, log_total)
    )
    key_value_grad = jnp.stack([key_grad, value_grad]).transpose(2, 0, 1, 3)
    key_value_grad = key_value_grad.reshape(context_count, rows, 2 * head_width)
    total = wide(key_value_grad[0])
    for rel in range(1, context_count):
        total = total + wide(swap(key_value_grad[rel], CT, rel))

    def turn_back(grad):
        return rotate(grad.reshape(rows, local_heads, head_dim), cosine, -sine_table).reshape(
            rows, head_width
        )

    query_norm_grad = turn_back(query_grad.transpose(1, 0, 2))
    key_norm_grad = turn_back(total[:, :head_width])
    gain_query_grad = jnp.sum(query_norm_grad * query_hat, 0)
    gain_key_grad = jnp.sum(key_norm_grad * key_hat, 0)
    query_hat_grad = query_norm_grad * gain_query_row
    key_hat_grad = key_norm_grad * gain_key_row
    inner = jnp.stack([jnp.sum(query_hat_grad * query_hat, -1), jnp.sum(key_hat_grad * key_hat, -1)])
    inner = sum(in_order(around(inner, TS), tensor_index))[:, :, None] / model_width
    query_low = low(scales[0] * (query_hat_grad - query_hat * inner[0]))
    key_low = low(scales[1] * (key_hat_grad - key_hat * inner[1]))
    qkv_low = jnp.concatenate([query_low, key_low, low(total[:, head_width:])], 1)
    qkv_blocks = jnp.concatenate(gather_groups(qkv_low), 0)
    attn_share = tensor_sum(tensor_parts(dot(qkv_low, qkv_weight, 1, 1)))
    qkv_w_grad = dot(jnp.concatenate(attn_slices, 0), qkv_blocks, 0, 0)
    hidden_share = wide(tokens.reshape(rows, quarter))
    normed_share = hidden_share * scale_attn
    normed_in_grad = attn_share * lax.dynamic_slice_in_dim(gain_attn, tensor_index * quarter, quarter)
    inner = jnp.sum(normed_in_grad * normed_share, -1)
    ends = jnp.concatenate([inner, jnp.sum(attn_share * normed_share, 0)])
    ends = in_order(around(ends, TS), tensor_index)
    inner = sum(end[:rows] for end in ends)[:, None] / model_width
    gain_attn_grad = jnp.concatenate([end[rows:] for end in ends])
    residual_grad_share = lax.dynamic_slice_in_dim(
        residual_grad, tensor_index * quarter, quarter, 1
    )
    tokens_grad = residual_grad_share + scale_attn * (normed_in_grad - normed_share * inner)

    gain_grads = jnp.stack([gain_query_grad, gain_key_grad]).reshape(
        2, local_heads, group_count, -1
    )
    gain_grads = gain_grads.transpose(2, 0, 1, 3).reshape(group_count, 2 * gain_size)
    vectors = jnp.concatenate(
        [
            gain_attn_grad.reshape(group_count, slice_width),
            gain_moe_grad.reshape(group_count, slice_width),
            gain_grads,
        ],
        1,
    )
    vectors = group_sum(
        jnp.concatenate(
            [
                lax.dynamic_slice_in_dim(vectors, group ^ rel, 1, 0)[:, None]
                for rel in range(group_count)
            ]
        )
    )[0]
    gain_grads = vectors[2 * slice_width :].reshape((2,) + q_gain.shape)
    return (
        mixed_out,
        tokens_grad.reshape(tokens.shape),
        vectors[:slice_width],
        qkv_w_grad[:, :head_width],
        qkv_w_grad[:, head_width : 2 * head_width],
        qkv_w_grad[:, 2 * head_width :],
        gain_grads[0],
        gain_grads[1],
        out_w_grad,
        vectors[slice_width : 2 * slice_width],
        router_grad,
        gate_w_grad,
        up_w_grad,
        down_grad,
    )


def solution(mesh):
    both = (SH, CT)
    rows = P(SH, CT, None, TS)
    pairs = P(SH, CT, None, None)
    vector, matrix, turned = P(both), P(both, TS), P(TS, both)
    up, down = P(both, None, TS), P(both, TS, None)
    return jax.shard_map(
        per_device,
        mesh=mesh,
        in_specs=(
            rows,
            P(SH, None),
            pairs,
            P(SH, CT, None),
            vector,
            matrix,
            matrix,
            matrix,
            turned,
            turned,
            turned,
            vector,
            P(both, None),
            up,
            up,
            down,
            rows,
        ),
        out_specs=(
            rows,
            rows,
            vector,
            matrix,
            matrix,
            matrix,
            turned,
            turned,
            turned,
            vector,
            P(both, None),
            up,
            up,
            down,
        ),
        check_vma=False,
    )
```

profile of v0, /device:TPU:8, one launch (start us, length us, event | category | flops | bytes accessed | tf_op | source)
XLA Modules:
  0.0 947.9 jit_solution(13955114688948421609)
XLA Ops:
  110.8 11.4 %collective-permute-done.5 = bf16[256,1664]{1,0:T(8,128)(2,1)} collective-permute-done((bf16[256,1664]{1,0:T(8,128)(2,1)}, bf16[256,1664]{1,0:T(8,128)(2,1)}, u32[]{:S(2)}, u32[]{:S(2)}) %collective-permute-start.5) | collective-permute-done | bytes 852000 | tf_op jit(solution)/shard_map/ppermute | solution.py:15
  127.9 15.8 %collective-permute-done.46 = bf16[256,2048]{1,0:T(8,128)(2,1)} collective-permute-done((bf16[256,2048]{1,0:T(8,128)(2,1)}, bf16[256,2048]{1,0:T(8,128)(2,1)}, u32[]{:S(2)}, u32[]{:S(2)}) %collective-permute-start.46) | collective-permute-done | bytes 1048608 | tf_op jit(solution)/shard_map/ppermute | solution.py:15
  148.9 17.9 %collective-permute-done.48 = bf16[256,2048]{1,0:T(8,128)(2,1)} collective-permute-done((bf16[256,2048]{1,0:T(8,128)(2,1)}, bf16[256,2048]{1,0:T(8,128)(2,1)}, u32[]{:S(2)}, u32[]{:S(2)}) %collective-permute-start.48) | collective-permute-done | bytes 1048608 | tf_op jit(solution)/shard_map/ppermute | solution.py:15
  237.0 18.4 %while.26 = (s32[]{:T(128)}, bf16[4,256,128]{1,2,0:T(8,128)(2,1)}, f32[4,256]{1,0:T(4,128)}, bf16[4,256,128]{2,1,0:T(8,128)(2,1)S(1)}, bf16[4,1024,128]{2,1,0:T(...) while((s32[]{:T(128)}, bf16[4,256,128]{1,2,0:T(8,128)(2,1)}, ...), condition=%wide.region_9.10_spmd, body=%wide.region_6.9_spmd.sunk | while | flops 136314624 | bytes 4145277 | solution.py:268
  269.2 11.8 %collective-permute-done.24 = bf16[256,512]{1,0:T(8,128)(2,1)S(1)} collective-permute-done((bf16[256,512]{1,0:T(8,128)(2,1)S(1)}, bf16[256,512]{1,0:T(8,128)(2,1)S(1)}, u32[]{:S(2)}, u32[]{:S(2)}) %collective-permute-start.24) | collective-permute-done | bytes 262176 | tf_op jit(solution)/shard_map/ppermute | solution.py:15
  281.0 13.7 %collective-permute-done.25 = bf16[256,512]{1,0:T(8,128)(2,1)S(1)} collective-permute-done((bf16[256,512]{1,0:T(8,128)(2,1)S(1)}, bf16[256,512]{1,0:T(8,128)(2,1)S(1)}, u32[]{:S(2)}, u32[]{:S(2)}) %collective-permute-start.25) | collective-permute-done | bytes 262176 | tf_op jit(solution)/shard_map/ppermute | solution.py:15
  313.7 20.2 %convolution_convert_fusion.4 = bf16[8,320,2048]{2,1,0:T(8,128)(2,1)} fusion(pred[8,320,256]{2,1,0:T(32,128)(4,1)S(1)} %bitcast_compare_fusion, bf16[8,256,2048]{2,1,0:T(8,128)(2,1)} %bitcast_dynamic-update-slice_fusion.7), kind=kOutput, calls=%fused_computation.84 | convolution fusion | flops 2689597440 | bytes 19529728 | tf_op jit(solution)/shard_map/dot_general | solution.py:300
  349.2 44.2 %collective-permute-done.37 = bf16[256,2176]{1,0:T(8,128)(2,1)S(1)} collective-permute-done((bf16[256,2176]{1,0:T(8,128)(2,1)S(1)}, bf16[256,2176]{1,0:T(8,128)(2,1)S(1)}, u32[]{:S(2)}, u32[]{:S(2)}) %collective-permute-start.37) | collective-permute-done | bytes 1114144 | tf_op jit(solution)/shard_map/ppermute | solution.py:15
  415.7 10.8 %fusion.50 = f32[8,8,40,256]{3,2,1,0:T(8,128)} fusion(bf16[8,2048,256]{2,1,0:T(8,128)(2,1)} %param.35, bf16[8,8,40,2176]{3,2,1,0:T(8,128)(2,1)} %bitcast.549), kind=kOutput, calls=%fused_computation.67 | convolution fusion | flops 2684354560 | bytes 21495808 | tf_op jit(solution)/shard_map/gekd,edf->gekf/dot_general | solution.py:315
  426.5 10.8 %fusion.54 = f32[8,8,40,256]{3,2,1,0:T(8,128)} fusion(bf16[8,2048,256]{2,1,0:T(8,128)(2,1)} %param.34, bf16[8,8,40,2176]{3,2,1,0:T(8,128)(2,1)} %bitcast.550), kind=kOutput, calls=%fused_computation.71 | convolution fusion | flops 2684354560 | bytes 21495808 | tf_op jit(solution)/shard_map/gekd,edf->gekf/dot_general | solution.py:315
  442.7 14.3 %fusion.84 = (f32[8,8,40]{2,0,1:T(8,128)S(1)}, bf16[8,8,40,256]{3,2,0,1:T(8,128)(2,1)}, bf16[8,8,40,256]{3,2,0,1:T(8,128)(2,1)}, bf16[8,8,40,256]{3,2,0,1:T(8,128)(2,1)}) fusion(f32[8,8,40,256]{3,2,1,0:T(8,128)} %fusion.50, f32[8,8,40,256]{3,2,1,0:T(8,128)} %fusion.54, f32[8,8,40]{2,0,1:T(8,128)S(1)} %fusion.109, bf16[8,256,2048]{2,1,0:T(8,128)(2,1)} %param.36, ...), kind=kOutput, calls=%fused_computation.103 | convolution fusion | flops 2696803840 | bytes 28069888 | tf_op jit(solution)/shard_map/gekd,efd->gekf/dot_general | solution.py:315
  458.3 13.3 %fusion.48 = f32[8,8,40,2048]{3,2,1,0:T(8,128)} fusion(bf16[8,8,40,256]{3,2,0,1:T(8,128)(2,1)S(1)} %copy-done.53, bf16[8,2048,256]{2,1,0:T(8,128)(2,1)} %param.35), kind=kOutput, calls=%fused_computation.65 | convolution fusion | flops 2684354560 | bytes 30670848 | tf_op jit(solution)/shard_map/gekf,edf->gekd/dot_general | solution.py:315
  471.6 15.6 %fusion.40 = bf16[8,8,40,2048]{3,2,0,1:T(8,128)(2,1)} fusion(f32[8,8,40,2048]{3,2,1,0:T(8,128)} %fusion.48, bf16[8,8,40,256]{3,2,0,1:T(8,128)(2,1)} %get-tuple-element.173, bf16[8,2048,256]{2,1,0:T(8,128)(2,1)} %param.34), kind=kOutput, calls=%fused_computation.54 | convolution fusion | flops 2694840320 | bytes 41156608 | tf_op jit(solution)/shard_map/gekf,edf->gekd/dot_general | solution.py:315
  487.2 16.6 %concatenate.147 = bf16[8,8,40,2176]{3,2,0,1:T(8,128)(2,1)} concatenate(bf16[8,8,40,2048]{3,2,0,1:T(8,128)(2,1)} %fusion.40, bf16[8,8,40,64]{3,2,0,1:T(8,128)(2,1)S(1)} %select_convert_fusion, bf16[8,8,40,64]{3,2,0,1:T(8,128)(2,1)S(1)} %fusion.108), dimensions={3} | concatenate | bytes 22282240 | tf_op jit(solution)/shard_map/concatenate | solution.py:330
  533.5 15.2 %fusion.62 = f32[8,2048,256]{2,1,0:T(8,128)} fusion(bf16[8,8,40,256]{3,2,0,1:T(8,128)(2,1)S(1)} %copy-done.55, bf16[8,8,40,2176]{3,2,1,0:T(8,128)(2,1)} %bitcast.551), kind=kOutput, calls=%fused_computation.81 | convolution fusion | flops 2684354560 | bytes 28573696 | tf_op jit(solution)/shard_map/gekd,gekf->edf/dot_general | solution.py:315
  560.0 15.5 %fusion.65 = f32[8,2048,256]{2,1,0:T(8,128)} fusion(bf16[8,8,40,256]{3,2,0,1:T(8,128)(2,1)S(1)} %copy-done.54, bf16[8,8,40,2176]{3,2,1,0:T(8,128)(2,1)} %bitcast.552), kind=kOutput, calls=%fused_computation.82 | convolution fusion | flops 2684354560 | bytes 28573696 | tf_op jit(solution)/shard_map/gekd,gekf->edf/dot_general | solution.py:315
  584.2 23.5 %collective-permute-done.55 = bf16[256,2176]{1,0:T(8,128)(2,1)} collective-permute-done((bf16[256,2176]{1,0:T(8,128)(2,1)}, bf16[256,2176]{1,0:T(8,128)(2,1)}, u32[]{:S(2)}, u32[]{:S(2)}) %collective-permute-start.55) | collective-permute-done | bytes 1114144 | tf_op jit(solution)/shard_map/ppermute | solution.py:15
  613.7 14.9 %fusion.68 = f32[8,256,2048]{2,1,0:T(8,128)} fusion(bf16[8,8,40,2048]{3,2,1,0:T(8,128)(2,1)} %bitcast.554, bf16[8,8,40,256]{3,2,0,1:T(8,128)(2,1)S(1)} %copy-done.52, f32[]{:T(128)} %bitcast.82, f32[8,8,40]{2,0,1:T(8,128)S(1)} %copy-done.72), kind=kOutput, calls=%fused_computation.83 | convolution fusion | flops 2686976000 | bytes 28583940 | tf_op jit(solution)/shard_map/gekf,gekd->efd/dot_general | solution.py:315
  707.0 20.7 %while.27 = (s32[]{:T(128)}, f32[4,256,128]{2,1,0:T(8,128)S(1)}, bf16[4,1024,128]{2,1,0:T(8,128)(2,1)}, bf16[4,1024,128]{2,1,0:T(8,128)(2,1)}, bf16[4,256,128]{2...) while((s32[]{:T(128)}, f32[4,256,128]{2,1,0:T(8,128)S(1)}, ...), condition=%wide.region_23.24_spmd, body=%wide.region_21.23_spmd.sunk | while | flops 338427648 | bytes 9840753 | solution.py:398
  748.1 13.5 %collective-permute-done.71 = bf16[256,1024]{1,0:T(8,128)(2,1)} collective-permute-done((bf16[256,1024]{1,0:T(8,128)(2,1)}, bf16[256,1024]{1,0:T(8,128)(2,1)}, u32[]{:S(2)}, u32[]{:S(2)}) %collective-permute-start.71) | collective-permute-done | bytes 524320 | tf_op jit(solution)/shard_map/ppermute | solution.py:15
  792.9 11.7 %collective-permute-done.77 = bf16[256,512]{1,0:T(8,128)(2,1)S(1)} collective-permute-done((bf16[256,512]{1,0:T(8,128)(2,1)S(1)}, bf16[256,512]{1,0:T(8,128)(2,1)S(1)}, u32[]{:S(2)}, u32[]{:S(2)}) %collective-permute-start.77) | collective-permute-done | bytes 262176 | tf_op jit(solution)/shard_map/ppermute | solution.py:15
  829.3 29.5 %collective-permute-done.91 = bf16[256,1536]{1,0:T(8,128)(2,1)S(1)} collective-permute-done((bf16[256,1536]{1,0:T(8,128)(2,1)}, bf16[256,1536]{1,0:T(8,128)(2,1)S(1)}, u32[]{:S(2)}, u32[]{:S(2)}) %collective-permute-start.91) | collective-permute-done | bytes 786464 | tf_op jit(solution)/shard_map/ppermute | solution.py:15
  875.7 20.6 %collective-permute-done.58 = bf16[256,2048]{1,0:T(8,128)(2,1)S(1)} collective-permute-done((bf16[256,2048]{1,0:T(8,128)(2,1)S(1)}, bf16[256,2048]{1,0:T(8,128)(2,1)S(1)}, u32[]{:S(2)}, u32[]{:S(2)}) %collective-permute-start.58) | collective-permute-done | bytes 1048608 | tf_op jit(solution)/shard_map/ppermute | solution.py:15
  896.2 21.0 %collective-permute-done.59 = bf16[256,2048]{1,0:T(8,128)(2,1)S(1)} collective-permute-done((bf16[256,2048]{1,0:T(8,128)(2,1)S(1)}, bf16[256,2048]{1,0:T(8,128)(2,1)S(1)}, u32[]{:S(2)}, u32[]{:S(2)}) %collective-permute-start.59) | collective-permute-done | bytes 1048608 | tf_op jit(solution)/shard_map/ppermute | solution.py:15
  (775 shorter events, 561.0 us)
Async XLA Ops:
  11.8 91.9 %collective-permute-start.3 = (bf16[256,1664]{1,0:T(8,128)(2,1)}, bf16[256,1664]{1,0:T(8,128)(2,1)}, u32[]{:S(2)}, u32[]{:S(2)}) collective-permute-start(bf16[256,1664]{1,0:T(8,128)(2,1)} %fusion.114), channel_id=1, source_target_pairs={{0,4},{4,0},{8,12},{12,8},{1,5},{5,1},{9,13},{13,9},{2,6},{6,2},{1... | collective-permute-start | bytes 2555912 | tf_op jit(solution)/shard_map/ppermute | solution.py:15
  28.8 77.9 %collective-permute-start.4 = (bf16[256,1664]{1,0:T(8,128)(2,1)}, bf16[256,1664]{1,0:T(8,128)(2,1)}, u32[]{:S(2)}, u32[]{:S(2)}) collective-permute-start(bf16[256,1664]{1,0:T(8,128)(2,1)} %fusion.114), channel_id=1, source_target_pairs={{0,8},{4,12},{8,0},{12,4},{1,9},{5,13},{9,1},{13,5},{2,10},{6,14},... | collective-permute-start | bytes 2555912 | tf_op jit(solution)/shard_map/ppermute | solution.py:15
  103.7 42.4 %collective-permute-start.47 = (bf16[256,2048]{1,0:T(8,128)(2,1)}, bf16[256,2048]{1,0:T(8,128)(2,1)}, u32[]{:S(2)}, u32[]{:S(2)}) collective-permute-start(bf16[256,2048]{1,0:T(8,128)(2,1)} %get-tuple-element.244), channel_id=1, source_target_pairs={{0,8},{4,12},{8,0},{12,4},{1,9},{5,13},{9,1},{13,5},{2,10},{6,14},... | collective-permute-start | bytes 3145736 | tf_op jit(solution)/shard_map/ppermute | solution.py:15
  106.7 60.1 %collective-permute-start.48 = (bf16[256,2048]{1,0:T(8,128)(2,1)}, bf16[256,2048]{1,0:T(8,128)(2,1)}, u32[]{:S(2)}, u32[]{:S(2)}) collective-permute-start(bf16[256,2048]{1,0:T(8,128)(2,1)} %get-tuple-element.244), channel_id=1, source_target_pairs={{0,12},{4,8},{8,4},{12,0},{1,13},{5,9},{9,5},{13,1},{2,14},{6,10},... | collective-permute-start | bytes 3145736 | tf_op jit(solution)/shard_map/ppermute | solution.py:15
  122.3 46.8 %collective-permute-start.49 = (bf16[256,2048]{1,0:T(8,128)(2,1)}, bf16[256,2048]{1,0:T(8,128)(2,1)}, u32[]{:S(2)}, u32[]{:S(2)}) collective-permute-start(bf16[256,2048]{1,0:T(8,128)(2,1)} %get-tuple-element.244), channel_id=1, source_target_pairs={{0,16},{16,0},{1,17},{17,1},{2,18},{18,2},{3,19},{19,3},{4,20},{20... | collective-permute-start | bytes 3145736 | tf_op jit(solution)/shard_map/ppermute | solution.py:15
  127.4 44.0 %collective-permute-start.7 = (bf16[256,1664]{1,0:T(8,128)(2,1)}, bf16[256,1664]{1,0:T(8,128)(2,1)S(1)}, u32[]{:S(2)}, u32[]{:S(2)}) collective-permute-start(bf16[256,1664]{1,0:T(8,128)(2,1)} %collective-permute-done.3), channel_id=1, source_target_pairs={{0,16},{16,0},{1,17},{17,1},{2,18},{18,2},{3,19},{19,3},{4,20},{20... | collective-permute-start | bytes 2555912 | tf_op jit(solution)/shard_map/ppermute | solution.py:15
  166.8 95.4 %collective-permute-start.50 = (bf16[256,2048]{1,0:T(8,128)(2,1)}, bf16[256,2048]{1,0:T(8,128)(2,1)}, u32[]{:S(2)}, u32[]{:S(2)}) collective-permute-start(bf16[256,2048]{1,0:T(8,128)(2,1)} %collective-permute-done.46), channel_id=1, source_target_pairs={{0,16},{16,0},{1,17},{17,1},{2,18},{18,2},{3,19},{19,3},{4,20},{20... | collective-permute-start | bytes 3145736 | tf_op jit(solution)/shard_map/ppermute | solution.py:15
  206.8 59.0 %collective-permute-start.51 = (bf16[256,2048]{1,0:T(8,128)(2,1)}, bf16[256,2048]{1,0:T(8,128)(2,1)}, u32[]{:S(2)}, u32[]{:S(2)}) collective-permute-start(bf16[256,2048]{1,0:T(8,128)(2,1)} %collective-permute-done.47), channel_id=1, source_target_pairs={{0,16},{16,0},{1,17},{17,1},{2,18},{18,2},{3,19},{19,3},{4,20},{20... | collective-permute-start | bytes 3145736 | tf_op jit(solution)/shard_map/ppermute | solution.py:15
  214.3 83.2 %collective-permute-start.52 = (bf16[256,2048]{1,0:T(8,128)(2,1)}, bf16[256,2048]{1,0:T(8,128)(2,1)}, u32[]{:S(2)}, u32[]{:S(2)}) collective-permute-start(bf16[256,2048]{1,0:T(8,128)(2,1)} %collective-permute-done.48), channel_id=1, source_target_pairs={{0,16},{16,0},{1,17},{17,1},{2,18},{18,2},{3,19},{19,3},{4,20},{20... | collective-permute-start | bytes 3145736 | tf_op jit(solution)/shard_map/ppermute | solution.py:15
  224.6 109.3 %collective-permute-start.87 = (bf16[2,256,256]{2,1,0:T(8,128)(2,1)}, bf16[2,256,256]{2,1,0:T(8,128)(2,1)}, u32[]{:S(2)}, u32[]{:S(2)}) collective-permute-start(bf16[2,256,256]{2,1,0:T(8,128)(2,1)} %get-tuple-element.219), channel_id=1, source_target_pairs={{0,4},{4,0},{8,12},{12,8},{1,5},{5,1},{9,13},{13,9},{2,6},{6,2},{1... | collective-permute-start | bytes 786440 | tf_op jit(solution)/shard_map/ppermute | solution.py:15
  268.9 67.3 %collective-permute-start.88 = (bf16[2,256,256]{2,1,0:T(8,128)(2,1)}, bf16[2,256,256]{2,1,0:T(8,128)(2,1)}, u32[]{:S(2)}, u32[]{:S(2)}) collective-permute-start(bf16[2,256,256]{2,1,0:T(8,128)(2,1)} %get-tuple-element.218), channel_id=1, source_target_pairs={{0,8},{4,12},{8,0},{12,4},{1,9},{5,13},{9,1},{13,5},{2,10},{6,14},... | collective-permute-start | bytes 786440 | tf_op jit(solution)/shard_map/ppermute | solution.py:15
  307.7 218.8 %collective-permute-start.97 = (bf16[256,512]{0,1:T(8,128)(2,1)}, bf16[256,512]{0,1:T(8,128)(2,1)S(1)}, u32[]{:S(2)}, u32[]{:S(2)}) collective-permute-start(bf16[256,512]{0,1:T(8,128)(2,1)} %bitcast.31), channel_id=1, source_target_pairs={{0,4},{4,0},{8,12},{12,8},{1,5},{5,1},{9,13},{13,9},{2,6},{6,2},{1... | collective-permute-start | bytes 786440 | tf_op jit(solution)/shard_map/ppermute | solution.py:15
  333.9 193.7 %collective-permute-start.98 = (bf16[256,512]{0,1:T(8,128)(2,1)}, bf16[256,512]{0,1:T(8,128)(2,1)S(1)}, u32[]{:S(2)}, u32[]{:S(2)}) collective-permute-start(bf16[256,512]{0,1:T(8,128)(2,1)} %bitcast.31), channel_id=1, source_target_pairs={{0,8},{4,12},{8,0},{12,4},{1,9},{5,13},{9,1},{13,5},{2,10},{6,14},... | collective-permute-start | bytes 786440 | tf_op jit(solution)/shard_map/ppermute | solution.py:15
  336.2 57.2 %collective-permute-start.37 = (bf16[256,2176]{1,0:T(8,128)(2,1)S(1)}, bf16[256,2176]{1,0:T(8,128)(2,1)S(1)}, u32[]{:S(2)}, u32[]{:S(2)}) collective-permute-start(bf16[256,2176]{1,0:T(8,128)(2,1)S(1)} %concatenate.145), channel_id=1, source_target_pairs={{0,8},{4,12},{8,0},{12,4},{1,9},{5,13},{9,1},{13,5},{2,10},{6,14},... | collective-permute-start | bytes 3342344 | tf_op jit(solution)/shard_map/ppermute | solution.py:15
  339.1 189.4 %collective-permute-start.99 = (bf16[256,512]{0,1:T(8,128)(2,1)}, bf16[256,512]{0,1:T(8,128)(2,1)}, u32[]{:S(2)}, u32[]{:S(2)}) collective-permute-start(bf16[256,512]{0,1:T(8,128)(2,1)} %bitcast.31), channel_id=1, source_target_pairs={{0,12},{4,8},{8,4},{12,0},{1,13},{5,9},{9,5},{13,1},{2,14},{6,10},... | collective-permute-start | bytes 786440 | tf_op jit(solution)/shard_map/ppermute | solution.py:15
  347.1 47.4 %collective-permute-start.38 = (bf16[256,2176]{1,0:T(8,128)(2,1)S(1)}, bf16[256,2176]{1,0:T(8,128)(2,1)S(1)}, u32[]{:S(2)}, u32[]{:S(2)}) collective-permute-start(bf16[256,2176]{1,0:T(8,128)(2,1)S(1)} %concatenate.145), channel_id=1, source_target_pairs={{0,12},{4,8},{8,4},{12,0},{1,13},{5,9},{9,5},{13,1},{2,14},{6,10},... | collective-permute-start | bytes 3342344 | tf_op jit(solution)/shard_map/ppermute | solution.py:15
  399.3 131.2 %collective-permute-start.100 = (bf16[256,512]{0,1:T(8,128)(2,1)}, bf16[256,512]{0,1:T(8,128)(2,1)S(1)}, u32[]{:S(2)}, u32[]{:S(2)}) collective-permute-start(bf16[256,512]{0,1:T(8,128)(2,1)} %bitcast.31), channel_id=1, source_target_pairs={{0,16},{16,0},{1,17},{17,1},{2,18},{18,2},{3,19},{19,3},{4,20},{20... | collective-permute-start | bytes 786440 | tf_op jit(solution)/shard_map/ppermute | solution.py:15
  557.9 49.8 %collective-permute-start.55 = (bf16[256,2176]{1,0:T(8,128)(2,1)}, bf16[256,2176]{1,0:T(8,128)(2,1)}, u32[]{:S(2)}, u32[]{:S(2)}) collective-permute-start(bf16[256,2176]{1,0:T(8,128)(2,1)} %get-tuple-element.180), channel_id=1, source_target_pairs={{0,8},{4,12},{8,0},{12,4},{1,9},{5,13},{9,1},{13,5},{2,10},{6,14},... | collective-permute-start | bytes 3342344 | tf_op jit(solution)/shard_map/ppermute | solution.py:15
  559.7 48.8 %collective-permute-start.56 = (bf16[256,2176]{1,0:T(8,128)(2,1)}, bf16[256,2176]{1,0:T(8,128)(2,1)}, u32[]{:S(2)}, u32[]{:S(2)}) collective-permute-start(bf16[256,2176]{1,0:T(8,128)(2,1)} %get-tuple-element.179), channel_id=1, source_target_pairs={{0,12},{4,8},{8,4},{12,0},{1,13},{5,9},{9,5},{13,1},{2,14},{6,10},... | collective-permute-start | bytes 3342344 | tf_op jit(solution)/shard_map/ppermute | solution.py:15
  666.4 197.9 %collective-permute-start.57 = (bf16[4,256,2048]{2,1,0:T(8,128)(2,1)}, bf16[4,256,2048]{2,1,0:T(8,128)(2,1)}, u32[]{:S(2)}, u32[]{:S(2)}) collective-permute-start(bf16[4,256,2048]{2,1,0:T(8,128)(2,1)} %slice.507), channel_id=1, source_target_pairs={{0,16},{16,0},{1,17},{17,1},{2,18},{18,2},{3,19},{19,3},{4,20},{20... | collective-permute-start | bytes 12582920 | tf_op jit(solution)/shard_map/ppermute | solution.py:15
  706.8 64.3 %collective-permute-start.104 = (bf16[4,256,256]{2,1,0:T(8,128)(2,1)}, bf16[4,256,256]{2,1,0:T(8,128)(2,1)}, u32[]{:S(2)}, u32[]{:S(2)}) collective-permute-start(bf16[4,256,256]{2,1,0:T(8,128)(2,1)} %pad_maximum_fusion.11), channel_id=1, source_target_pairs={{0,16},{16,0},{1,17},{17,1},{2,18},{18,2},{3,19},{19,3},{4,20},{20... | collective-permute-start | bytes 1572872 | tf_op jit(solution)/shard_map/ppermute | solution.py:15
  783.1 44.7 %collective-permute-start.90 = (bf16[256,1536]{1,0:T(8,128)(2,1)}, bf16[256,1536]{1,0:T(8,128)(2,1)S(1)}, u32[]{:S(2)}, u32[]{:S(2)}) collective-permute-start(bf16[256,1536]{1,0:T(8,128)(2,1)} %get-tuple-element.250), channel_id=1, source_target_pairs={{0,4},{4,0},{8,12},{12,8},{1,5},{5,1},{9,13},{13,9},{2,6},{6,2},{1... | collective-permute-start | bytes 2359304 | tf_op jit(solution)/shard_map/ppermute | solution.py:15
  871.6 45.6 %collective-permute-start.59 = (bf16[256,2048]{1,0:T(8,128)(2,1)S(1)}, bf16[256,2048]{1,0:T(8,128)(2,1)S(1)}, u32[]{:S(2)}, u32[]{:S(2)}) collective-permute-start(bf16[256,2048]{1,0:T(8,128)(2,1)S(1)} %get-tuple-element.183), channel_id=1, source_target_pairs={{0,8},{4,12},{8,0},{12,4},{1,9},{5,13},{9,1},{13,5},{2,10},{6,14},... | collective-permute-start | bytes 3145736 | tf_op jit(solution)/shard_map/ppermute | solution.py:15
  872.4 46.5 %collective-permute-start.60 = (bf16[256,2048]{1,0:T(8,128)(2,1)S(1)}, bf16[256,2048]{1,0:T(8,128)(2,1)S(1)}, u32[]{:S(2)}, u32[]{:S(2)}) collective-permute-start(bf16[256,2048]{1,0:T(8,128)(2,1)S(1)} %get-tuple-element.182), channel_id=1, source_target_pairs={{0,12},{4,8},{8,4},{12,0},{1,13},{5,9},{9,5},{13,1},{2,14},{6,10},... | collective-permute-start | bytes 3145736 | tf_op jit(solution)/shard_map/ppermute | solution.py:15
  (195 other events, 2551.6 us)
where the time goes:
time: 951 us; the launch traced here: 948 us
  waiting for transfers between devices  363 us (38%)
  matrix products  213 us (22%)
  local copies, waits for them, and re-layouts  196 us (21%)
  starting transfers between devices  104 us (11%)
  other arithmetic  67 us (7%)
    ppermute x115, waiting for transfers between devices, swap(): return lax.ppermute(value, axis, [(i, i ^ rel) for i in range(count)])  363 us
    dot_general x9, matrix products, by_expert(): return jnp.einsum(spec, left, right, preferred_element_type=F32)  119 us
    ppermute x115, starting transfers between devices, swap(): return lax.ppermute(value, axis, [(i, i ^ rel) for i in range(count)])  104 us
    dot_general x37, matrix products, dot(): lax.dot_general(left, right, (((left_dim,), (right_dim,)), ((), ())), pre...  49.9 us
    unnamed x245, local copies, waits for them, and re-layouts  41 us
    dynamic_update_slice x16, local copies, waits for them, and re-layouts, stack_blocks(): whole = lax.dynamic_update_index_in_dim(whole, block, rel, 0)  32.7 us
    concatenate x2, local copies, waits for them, and re-layouts, per_device(): returned = jnp.concatenate([row_grads] + split_low(dots), -1)  22.3 us
    dot_general x1, matrix products, per_device(): lax.dot_general(choose, grad_blocks, batched, preferred_element_type=F32)  20.2 us
  transfers between devices with their start and end apart: 115, of which 50 were waited for; matrix products, arithmetic and copies ran while one was open for 44% of the time, Pallas kernels for 0%

commit v1 on v0

v1 whole, which is shorter than its diff:
```python
import functools

import jax
import jax.numpy as jnp
from jax import lax
from jax.experimental import pallas as pl
from jax.experimental.pallas import tpu as pltpu
from jax.sharding import PartitionSpec as P

EPS = 1e-05
ROPE_BASE = 10000.0
NEG_FILL = -1e30
SH, CT, TS = "shard", "context", "tensor"
F32, BF16 = jnp.float32, jnp.bfloat16
CHUNK = 512
VMEM_BYTES = 58 * 2**20


def swap(value, axis, rel):
    count = lax.axis_size(axis)
    return lax.ppermute(value, axis, [(i, i ^ rel) for i in range(count)])


def around(value, axis):
    return [value] + [swap(value, axis, rel) for rel in range(1, lax.axis_size(axis))]


def gather_context(value, *middle):
    half = value.shape[0] // 2
    if lax.axis_size(CT) != 4 or half % 16:
        return around(value, CT)
    first, second = hold(swap(value, CT, 1), *middle), hold(swap(value, CT, 2), *middle)
    third = [swap(first[:half], CT, 2), swap(second[half:], CT, 1)]
    return [value, first, second, jnp.concatenate(third)]


def gather_groups(value, *middle):
    blocks = gather_context(value, *middle)
    for rel in range(1, lax.axis_size(SH)):
        blocks = blocks + [swap(block, SH, rel) for block in blocks[: lax.axis_size(CT)]]
    return blocks


def stack_far(blocks):
    far = [swap(jnp.stack(blocks), SH, rel) for rel in range(1, lax.axis_size(SH))]
    return blocks + [(one, place) for one in far for place in range(len(blocks))]


def plain(block):
    return block[0][block[1]] if isinstance(block, tuple) else block


def array_of(block):
    return block[0] if isinstance(block, tuple) else block


def block_spec(block, size, column):
    if isinstance(block, tuple):
        array, place = block
        return pl.BlockSpec((None, array.shape[1], size), lambda i: (place, 0, column))
    return pl.BlockSpec((block.shape[0], size), lambda i: (0, column))


def butterfly(value, axis):
    rel = 1
    while rel < lax.axis_size(axis):
        value = value + swap(value, axis, rel)
        rel *= 2
    return value


def double(value, axis):
    rel = 1
    while rel < lax.axis_size(axis):
        value = jnp.concatenate([value, swap(value, axis, rel)])
        rel *= 2
    return value


def in_order(blocks, index):
    ordered = []
    for place in range(len(blocks)):
        picked = blocks[place]
        for mine in range(1, len(blocks)):
            picked = jnp.where(index == mine, blocks[place ^ mine], picked)
        ordered.append(picked)
    return ordered


def place_rows(blocks, index):
    rows = blocks[0].shape[0]
    whole = jnp.zeros((rows * len(blocks),) + blocks[0].shape[1:], blocks[0].dtype)
    for rel, block in enumerate(blocks):
        whole = lax.dynamic_update_slice_in_dim(whole, block, (index ^ rel) * rows, 0)
    return whole


def low(value):
    return value.astype(BF16)


def wide(value):
    return value.astype(F32)


def hold_kernel(*refs):
    pass


def hold(value, *others):
    if not others:
        return value
    anywhere = pl.BlockSpec(memory_space=pl.ANY)
    return pl.pallas_call(
        hold_kernel,
        out_shape=jax.ShapeDtypeStruct(value.shape, value.dtype),
        in_specs=[anywhere] * (1 + len(others)),
        out_specs=anywhere,
        input_output_aliases={0: 0},
        cost_estimate=pl.CostEstimate(flops=0, bytes_accessed=0, transcendentals=0),
    )(value, *others)


def dot(left, right, left_dim=1, right_dim=0):
    return lax.dot_general(
        left, right, (((left_dim,), (right_dim,)), ((), ())), preferred_element_type=F32
    )


def joint(values, *others):
    first = hold(values[0], *values[1:], *others)
    return [first] + [hold(value, first) for value in values[1:]]


def core_sum(other, mine):
    came = [swap(block, SH, 1) for block in other]
    return [(block, one) for block, one in zip(mine, came)]


def add_up(blocks, cut=slice(None)):
    return sum(wide(block[cut]) for block in blocks)


def context_start(mine):
    half = mine[0][0].shape[0] // 2
    if len(mine) != 4 or half % 16:
        return [swap(low(add_up(blocks)), CT, rel) for rel, blocks in enumerate(mine) if rel]
    top, bottom = slice(0, half), slice(half, None)
    upper = [low(add_up(mine[1], top)), low(add_up(mine[3], top))]
    lower = [low(add_up(mine[2], bottom)), low(add_up(mine[3], bottom))]
    return [swap(jnp.stack(upper), CT, 1), swap(jnp.stack(lower), CT, 2)]


def context_end(mine, came, *middle):
    half = mine[0][0].shape[0] // 2
    if len(mine) != 4 or half % 16:
        return add_up(mine[0]) + sum(wide(block) for block in came)
    top, bottom = slice(0, half), slice(half, None)
    upper, lower = joint(came, *middle)
    pass_upper = low(add_up(mine[2], top) + wide(upper[1]))
    pass_lower = low(add_up(mine[1], bottom) + wide(lower[1]))
    upper = add_up(mine[0], top) + wide(upper[0]) + wide(swap(pass_upper, CT, 2))
    lower = add_up(mine[0], bottom) + wide(lower[0]) + wide(swap(pass_lower, CT, 1))
    return jnp.concatenate([upper, lower])


def trade_start(stacked, *middle):
    shard_count, context_count = lax.axis_size(SH), lax.axis_size(CT)
    parts = [stacked[:context_count]]
    for rel in range(1, shard_count):
        parts.append(swap(stacked[rel * context_count : (rel + 1) * context_count], SH, rel))
    parts = jnp.stack(parts)
    return [parts[:, 0]] + [
        swap(hold(parts[:, rel], *middle), CT, rel) for rel in range(1, context_count)
    ]


def tree_info(parent_row):
    slot_count = parent_row.shape[0]
    slot_ids = jnp.arange(slot_count, dtype=jnp.int32)
    reach = (parent_row[:, None] == slot_ids[None, :]) | (slot_ids[:, None] == slot_ids[None, :])
    span = 1
    while span < slot_count:
        reach = jnp.any(reach[:, :, None] & reach[None, :, :], 1)
        span *= 2
    depths = jnp.sum(reach.astype(jnp.int32), 1) - 1
    return (reach, depths)


def rope_tables(positions, head_dim):
    half_dim = head_dim // 2
    frequency = ROPE_BASE ** (-2.0 * jnp.arange(half_dim, dtype=F32) / head_dim)
    angles = positions.astype(F32)[:, None] * frequency[None, :]
    cosine = jnp.concatenate([jnp.cos(angles), jnp.cos(angles)], -1)
    return (cosine, jnp.concatenate([-jnp.sin(angles), jnp.sin(angles)], -1))


def own_slots(chosen, order, first_expert, expert_dev, capacity):
    expert_ids = first_expert + jnp.arange(expert_dev, dtype=jnp.int32)
    hit = chosen[:, :, :, None] == expert_ids
    rank = jnp.sum(jnp.where(hit, order[:, :, :, None], 0), 2)
    routed = jnp.any(hit, 2)
    rank = jnp.where(routed, rank, 2**30).transpose(0, 2, 1)
    routed = routed.transpose(0, 2, 1)
    place = jnp.sum((rank[:, :, None, :] < rank[:, :, :, None]).astype(jnp.int32), -1)
    return jnp.where(routed & (place < capacity), place, -1)


def split_low(value):
    high = low(value)
    return [high, low(value - wide(high))]


def compiler_params():
    return pltpu.CompilerParams(vmem_limit_bytes=VMEM_BYTES)


def cost(microseconds):
    return pl.CostEstimate(
        flops=int(microseconds * 1e9), bytes_accessed=0, transcendentals=0
    )


def column_chunks(width):
    starts = list(range(0, width, CHUNK))
    return [slice(start, min(start + CHUNK, width)) for start in starts]


def choose_matrix(slots, pad):
    count, rows = slots.shape
    places = lax.broadcasted_iota(jnp.int32, (pad, rows), 0)
    parts = [
        jnp.where(slots[one : one + 1, :] == places, 1.0, 0.0) for one in range(count)
    ]
    return low(jnp.concatenate(parts, 0))


def choose_turned(slots, pad):
    count, rows = slots.shape
    expert = lax.broadcasted_iota(jnp.int32, (count, count * pad), 0)
    column = lax.broadcasted_iota(jnp.int32, (count, count * pad), 1)
    inside = (column >= expert * pad) & (column < (expert + 1) * pad)
    spread = dot(low(slots), low(jnp.where(inside, 1.0, 0.0)), 0, 0)
    place = jnp.sum(jnp.where(inside, column - expert * pad, 0), 0, keepdims=True)
    return low(jnp.where(spread == wide(place), 1.0, 0.0))


def load_block(step, blocks, buffer, sems):
    slots = buffer.shape[0]

    def copy(rel):
        return pltpu.make_async_copy(blocks[rel], buffer.at[rel % slots], sems.at[rel % slots])

    for rel in range(len(blocks)):

        @pl.when(step == rel)
        def _():
            if rel == 0:
                for ahead in range(min(slots, len(blocks)) - 1):
                    copy(ahead).start()
            if rel + slots - 1 < len(blocks):
                copy(rel + slots - 1).start()
            copy(rel).wait()


def split_refs(refs):
    parts = []
    for ref in refs:
        parts += [ref] if len(ref.shape) == 2 else [ref.at[one] for one in range(ref.shape[0])]
    return parts


def dispatch_kernel(pad, slots_ref, *refs):
    *blocks, out_ref, buffer, sems = refs
    blocks = split_refs(blocks)
    step = pl.program_id(0)
    load_block(step, blocks, buffer, sems)
    choose = choose_matrix(slots_ref[0], pad)
    count = slots_ref.shape[1]
    for cut in column_chunks(buffer.shape[2]):
        picked = low(dot(choose, buffer[lax.rem(step, buffer.shape[0]), :, cut]))
        for one in range(count):
            out_ref[one, 0, :, cut] = picked[one * pad : (one + 1) * pad]


def dispatch(slots, blocks, pad):
    group_count, expert_dev, rows = slots.shape
    width = blocks[0].shape[1]
    blocks = [array_of(block) for block in blocks if array_of(block) is block or block[1] == 0]
    return pl.pallas_call(
        functools.partial(dispatch_kernel, pad),
        grid=(group_count,),
        out_shape=jax.ShapeDtypeStruct((expert_dev, group_count, pad, width), BF16),
        in_specs=[pl.BlockSpec((1, expert_dev, rows), lambda i: (i, 0, 0))]
        + [pl.BlockSpec(memory_space=pl.ANY)] * len(blocks),
        out_specs=pl.BlockSpec((expert_dev, 1, pad, width), lambda i: (0, i, 0, 0)),
        scratch_shapes=[pltpu.VMEM((4, rows, width), BF16), pltpu.SemaphoreType.DMA((4,))],
        compiler_params=compiler_params(),
        cost_estimate=cost(12),
    )(slots, *blocks)


def combine_all(slots_ref, scratch, pad, outs, buffer, sems):
    count, pair_rows, width = scratch.shape
    group_count = len(outs)

    def copy(turn, source):
        return pltpu.make_async_copy(buffer.at[turn % 2], outs[source], sems.at[turn % 2])

    def body(turn, carry):
        source = lax.rem(turn + group_count // 2, group_count)
        choose = choose_turned(slots_ref[source], pad)
        start = pl.multiple_of(source * pad, pad)

        @pl.when(turn >= 2)
        def _():
            copy(turn, 0).wait()

        for cut in column_chunks(width):
            picked = scratch[:, pl.ds(start, pad), cut].reshape(count * pad, cut.stop - cut.start)
            buffer[turn % 2, :, cut] = low(dot(choose, picked))

        for one in range(group_count):

            @pl.when(source == one)
            def _():
                copy(turn, one).start()

        return carry

    lax.fori_loop(0, group_count, body, 0)
    for turn in range(group_count - 2, group_count):
        copy(turn, 0).wait()


def experts_kernel(
    group_count,
    pad,
    pieces,
    expert_count,
    first_ref,
    slots_ref,
    grads_ref,
    gate_ref,
    up_ref,
    down_ref,
    *refs,
):
    blocks = refs[:group_count]
    rows_out, act_out, back_out = refs[group_count : group_count + 3]
    outs = refs[group_count + 3 : 2 * group_count + 3]
    buffer, row_scratch, back_scratch, gate_scratch, sems, out_sems = refs[2 * group_count + 3 :]
    expert_dev, pair_rows, width = row_scratch.shape
    piece_rows = pair_rows // pieces
    hidden = gate_ref.shape[2]
    step = pl.program_id(0)

    def out_copy(one):
        return pltpu.make_async_copy(row_scratch.at[one], rows_out.at[one], out_sems.at[one])

    def pick(source, carry):
        load_block(source, blocks, buffer, sems)
        choose = choose_matrix(slots_ref[source], pad)
        start = pl.multiple_of(source * pad, pad)
        for cut in column_chunks(width):
            picked = low(dot(choose, buffer[lax.rem(source, buffer.shape[0]), :, cut]))
            for one in range(expert_dev):
                row_scratch[one, pl.ds(start, pad), cut] = picked[one * pad : (one + 1) * pad]
        gates = dot(choose, buffer[lax.rem(source, buffer.shape[0]), :, width:])
        gates = gates[:, :expert_count] + gates[:, expert_count:]
        column = lax.broadcasted_iota(jnp.int32, (pad, expert_count), 1)
        for one in range(expert_dev):
            own = column == first_ref[0] + one
            gate_scratch[one, pl.ds(start, pad), :] = jnp.sum(
                jnp.where(own, gates[one * pad : (one + 1) * pad], 0.0), -1, keepdims=True
            )
        return carry

    @pl.when(step == 0)
    def _():
        lax.fori_loop(0, group_count, pick, 0)

    one = step // pieces
    start = pl.multiple_of(lax.rem(step, pieces) * piece_rows, piece_rows)
    span = pl.ds(start, piece_rows)

    @pl.when(start == 0)
    def _():
        out_copy(one).start()

    rows = row_scratch[one, span, :]
    gate_proj = dot(rows, gate_ref[0])
    up_proj = dot(rows, up_ref[0])
    act_raw = dot(grads_ref[0], down_ref[0], 1, 1)
    gates = gate_scratch[one, span, :]
    sigmoid_gate = 1.0 / (1.0 + jnp.exp(-gate_proj))
    silu_gate = gate_proj * sigmoid_gate
    activated = wide(low(silu_gate * up_proj))
    dots = jnp.sum(activated * act_raw, -1, keepdims=True)
    act_grad = act_raw * gates
    gate_low = low(act_grad * up_proj * sigmoid_gate * (1.0 + gate_proj * (1.0 - sigmoid_gate)))
    up_low = low(act_grad * silu_gate)
    act_out[0] = low(activated * gates)
    back_out[0, :, :hidden] = gate_low
    back_out[0, :, hidden:] = up_low
    for cut in column_chunks(width):
        back_scratch[one, span, cut] = low(
            dot(gate_low, gate_ref[0, cut, :], 1, 1) + dot(up_low, up_ref[0, cut, :], 1, 1)
        )
    column = lax.broadcasted_iota(jnp.int32, (piece_rows, expert_count), 1)
    spread = jnp.where(column == first_ref[0] + one, dots, 0.0)
    back_scratch[one, span, width:] = jnp.concatenate(split_low(spread), 1)

    @pl.when(step == expert_dev * pieces - 1)
    def _():
        combine_all(slots_ref, back_scratch, pad, outs, buffer, sems)
        for one in range(expert_dev):
            out_copy(one).wait()


def experts(first, slots, blocks, grad_rows, w_gate, w_up, w_down, pad, expert_count):
    group_count, expert_dev, rows = slots.shape
    _, width, hidden = w_gate.shape
    pair_rows = group_count * pad
    pieces = max(1, pair_rows // 384)
    piece_rows = pair_rows // pieces
    full = blocks[0].shape[1]
    whole = pl.BlockSpec(slots.shape, lambda i: (0, 0, 0))
    into = pl.BlockSpec((1, width, hidden), lambda i: (i // pieces, 0, 0))
    onto = pl.BlockSpec((1, hidden, width), lambda i: (i // pieces, 0, 0))

    def piece(size):
        return pl.BlockSpec((1, piece_rows, size), lambda i: (i // pieces, lax.rem(i, pieces), 0))

    pairs = expert_dev * pair_rows
    return pl.pallas_call(
        functools.partial(experts_kernel, group_count, pad, pieces, expert_count),
        grid=(expert_dev * pieces,),
        out_shape=[
            jax.ShapeDtypeStruct((expert_dev, pair_rows, size), BF16)
            for size in (width, hidden, 2 * hidden)
        ]
        + [jax.ShapeDtypeStruct((rows, full), BF16)] * group_count,
        in_specs=[pl.BlockSpec(memory_space=pltpu.SMEM), whole, piece(width), into, into, onto]
        + [pl.BlockSpec(memory_space=pl.ANY)] * group_count,
        out_specs=[pl.BlockSpec(memory_space=pl.ANY), piece(hidden), piece(2 * hidden)]
        + [pl.BlockSpec(memory_space=pl.ANY)] * group_count,
        scratch_shapes=[
            pltpu.VMEM((4, rows, full), BF16),
            pltpu.VMEM((expert_dev, pair_rows, width), BF16),
            pltpu.VMEM((expert_dev, pair_rows, full), BF16),
            pltpu.VMEM((expert_dev, pair_rows, 1), F32),
            pltpu.SemaphoreType.DMA((4,)),
            pltpu.SemaphoreType.DMA((expert_dev,)),
        ],
        compiler_params=compiler_params(),
        cost_estimate=cost(100),
    )(first, slots, grad_rows, w_gate, w_up, w_down, *blocks)


def expert_out_kernel(pad, pieces, skip, slots_ref, act_ref, down_ref, *refs):
    outs, (scratch, buffer, sems) = split_refs(refs[skip:-3]), refs[-3:]
    expert_dev, pair_rows, width = scratch.shape
    piece_rows = pair_rows // pieces
    step = pl.program_id(0)
    start = pl.multiple_of(lax.rem(step, pieces) * piece_rows, piece_rows)
    for cut in column_chunks(width):
        scratch[step // pieces, pl.ds(start, piece_rows), cut] = low(
            dot(act_ref[0], down_ref[0, :, cut])
        )

    @pl.when(step == expert_dev * pieces - 1)
    def _():
        combine_all(slots_ref, scratch, pad, outs, buffer, sems)


def expert_out(slots, act, w_down, pad, near, *earlier):
    group_count, expert_dev, rows = slots.shape
    _, hidden, width = w_down.shape
    pair_rows = group_count * pad
    pieces = max(1, pair_rows // 384)
    pairs = expert_dev * pair_rows
    return pl.pallas_call(
        functools.partial(expert_out_kernel, pad, pieces, len(earlier)),
        grid=(expert_dev * pieces,),
        out_shape=[jax.ShapeDtypeStruct((rows, width), BF16)] * near
        + [jax.ShapeDtypeStruct((group_count - near, rows, width), BF16)],
        in_specs=[
            pl.BlockSpec(slots.shape, lambda i: (0, 0, 0)),
            pl.BlockSpec(
                (1, pair_rows // pieces, hidden), lambda i: (i // pieces, lax.rem(i, pieces), 0)
            ),
            pl.BlockSpec((1, hidden, width), lambda i: (i // pieces, 0, 0)),
        ]
        + [pl.BlockSpec(memory_space=pl.ANY)] * len(earlier),
        out_specs=[pl.BlockSpec(memory_space=pl.ANY)] * (near + 1),
        scratch_shapes=[
            pltpu.VMEM((expert_dev, pair_rows, width), BF16),
            pltpu.VMEM((2, rows, width), BF16),
            pltpu.SemaphoreType.DMA((2,)),
        ],
        compiler_params=compiler_params(),
        cost_estimate=cost(40),
    )(slots, act, w_down, *earlier)


def weight_grad_kernel(pieces, skip, left_ref, right_ref, *outs):
    outs = outs[skip:]
    inside = lax.rem(pl.program_id(0), pieces)
    size = outs[0].shape[2]
    tall = left_ref.shape[2] >= right_ref.shape[2]

    def add(out_ref, index, term):
        if pieces == 1:
            out_ref[index] = term
        else:

            @pl.when(inside == 0)
            def _():
                out_ref[index] = term

            @pl.when(inside > 0)
            def _():
                out_ref[index] += term

    if tall:
        for cut in column_chunks(left_ref.shape[2]):
            term = dot(left_ref[0, :, cut], right_ref[0], 0, 0)
            for one, out_ref in enumerate(outs):
                add(out_ref, (0, cut), term[:, one * size : (one + 1) * size])
    else:
        for cut in column_chunks(right_ref.shape[2]):
            add(outs[0], (0, slice(None), cut), dot(left_ref[0], right_ref[0, :, cut], 0, 0))


def weight_grad(left, right, count, *earlier):
    expert_dev, pair_rows, tall = left.shape
    size = right.shape[2] // count
    pieces = max(1, pair_rows // 384)

    def piece(width):
        return pl.BlockSpec(
            (1, pair_rows // pieces, width), lambda i: (i // pieces, lax.rem(i, pieces), 0)
        )

    return pl.pallas_call(
        functools.partial(weight_grad_kernel, pieces, len(earlier)),
        grid=(expert_dev * pieces,),
        out_shape=[jax.ShapeDtypeStruct((expert_dev, tall, size), F32)] * count,
        in_specs=[piece(tall), piece(right.shape[2])]
        + [pl.BlockSpec(memory_space=pl.ANY)] * len(earlier),
        out_specs=[pl.BlockSpec((1, tall, size), lambda i: (i // pieces, 0, 0))] * count,
        compiler_params=compiler_params(),
        cost_estimate=cost(80),
    )(left, right, *earlier)


def scatter_dot_kernel(index_ref, value_ref, *refs):
    blocks, out_ref = refs[:-1], refs[-1]
    depth = blocks[0].shape[0]
    for rel, block in enumerate(blocks):
        start = pl.multiple_of((index_ref[0] ^ rel) * depth, depth)
        part = dot(value_ref[...], block[...], 1, 1)
        out_ref[:, pl.ds(start, depth)] = part.astype(out_ref.dtype)


def scatter_dot(index, value, blocks, cut, kind):
    rows = value.shape[0]
    depth = blocks[0].shape[0]
    size = cut.stop - cut.start
    if depth % 128:
        whole = place_rows([plain(block)[:, cut] for block in blocks], index)
        return dot(value, whole, 1, 1).astype(kind)
    first = cut.start // size
    return pl.pallas_call(
        scatter_dot_kernel,
        grid=(1,),
        out_shape=jax.ShapeDtypeStruct((rows, depth * len(blocks)), kind),
        in_specs=[
            pl.BlockSpec(memory_space=pltpu.SMEM),
            pl.BlockSpec((rows, size), lambda i: (0, 0)),
        ]
        + [block_spec(block, size, first) for block in blocks],
        out_specs=pl.BlockSpec((rows, depth * len(blocks)), lambda i: (0, 0)),
        compiler_params=compiler_params(),
        cost_estimate=cost(12),
    )(index.reshape(1), value, *[array_of(block) for block in blocks])


def attend_kernel(score_scale, context_count, query_ref, bias_ref, *refs):
    blocks = refs[:context_count]
    out_ref, total_ref = refs[context_count:]
    head_dim = query_ref.shape[1]
    scores = jnp.concatenate(
        [dot(query_ref[...], block[:, :head_dim], 1, 1) for block in blocks], 1
    )
    scores = scores * score_scale + bias_ref[...]
    row_peak = jnp.max(scores, -1, keepdims=True)
    weights = jnp.exp(scores - row_peak)
    row_total = jnp.sum(weights, -1, keepdims=True)
    probabilities = low(weights / row_total)
    rows = query_ref.shape[0]
    attended = sum(
        dot(probabilities[:, rel * rows : (rel + 1) * rows], block[:, head_dim:])
        for rel, block in enumerate(blocks)
    )
    out_ref[...] = low(attended)
    total_ref[0] = row_peak + jnp.log(row_total)


def attend(queries, blocks, bias, head_dim):
    rows, head_width = queries.shape
    heads = head_width // head_dim
    one = pl.BlockSpec((rows, head_dim), lambda h: (0, h))
    two = pl.BlockSpec((rows, 2 * head_dim), lambda h: (0, h))
    return pl.pallas_call(
        functools.partial(attend_kernel, head_dim ** (-0.5), len(blocks)),
        grid=(heads,),
        out_shape=[
            jax.ShapeDtypeStruct((rows, head_width), BF16),
            jax.ShapeDtypeStruct((heads, rows, 1), F32),
        ],
        in_specs=[one, pl.BlockSpec(bias.shape, lambda h: (0, 0))] + [two] * len(blocks),
        out_specs=[one, pl.BlockSpec((1, rows, 1), lambda h: (h, 0, 0))],
        compiler_params=compiler_params(),
        cost_estimate=cost(12),
    )(queries, bias, *blocks)


def attend_back_kernel(score_scale, context_count, query_ref, grad_ref, total_ref, bias_ref, *refs):
    blocks = refs[:context_count]
    query_out, outs = refs[context_count], refs[context_count + 1 :]
    rows, head_dim = query_ref.shape
    query, grad = query_ref[...], grad_ref[...]
    scores = jnp.concatenate([dot(query, block[:, :head_dim], 1, 1) for block in blocks], 1)
    probabilities = jnp.exp(scores * score_scale + bias_ref[...] - total_ref[0])
    prob_grad = jnp.concatenate([dot(grad, block[:, head_dim:], 1, 1) for block in blocks], 1)
    score_grad = probabilities * (
        prob_grad - jnp.sum(probabilities * prob_grad, -1, keepdims=True)
    )
    score_low = low(score_grad * score_scale)
    prob_low = low(probabilities)
    query_grad = jnp.zeros((rows, head_dim), F32)
    for rel, (block, out) in enumerate(zip(blocks, outs)):
        cut = slice(rel * rows, (rel + 1) * rows)
        query_grad = query_grad + dot(score_low[:, cut], block[:, :head_dim])
        out[:, :head_dim] = low(dot(score_low[:, cut], query, 0, 0))
        out[:, head_dim:] = low(dot(prob_low[:, cut], grad, 0, 0))
    query_out[...] = query_grad


def attend_back(queries, grads, totals, blocks, bias, head_dim):
    rows, head_width = queries.shape
    heads = head_width // head_dim
    one = pl.BlockSpec((rows, head_dim), lambda h: (0, h))
    two = pl.BlockSpec((rows, 2 * head_dim), lambda h: (0, h))
    return pl.pallas_call(
        functools.partial(attend_back_kernel, head_dim ** (-0.5), len(blocks)),
        grid=(heads,),
        out_shape=[jax.ShapeDtypeStruct((rows, head_width), F32)]
        + [jax.ShapeDtypeStruct((rows, 2 * head_width), BF16)] * len(blocks),
        in_specs=[
            one,
            one,
            pl.BlockSpec((1, rows, 1), lambda h: (h, 0, 0)),
            pl.BlockSpec(bias.shape, lambda h: (0, 0)),
        ]
        + [two] * len(blocks),
        out_specs=[one] + [two] * len(blocks),
        compiler_params=compiler_params(),
        cost_estimate=cost(12),
    )(queries, grads, totals, bias, *blocks)


def row_norm(values):
    return lax.rsqrt(jnp.mean(values * values, -1, keepdims=True) + EPS)


def chunk(index_ref, rel, size):
    return pl.ds(pl.multiple_of((index_ref[0] ^ rel) * size, size), size)


def whole_spec(value):
    return pl.BlockSpec(value.shape, lambda i: (0,) * value.ndim)


def column_spec(value, size, first=0):
    return pl.BlockSpec((value.shape[0], size), lambda i: (0, first + i))


def project_kernel(group_count, heads, index_ref, hidden_ref, *refs):
    smalls, blocks = refs[:group_count], refs[group_count : 2 * group_count]
    attn_ref, out_ref, square_ref, scale_ref, moe_ref, gain_ref = refs[2 * group_count :]
    depth = blocks[0].shape[0]
    piece = gain_ref.shape[1] // (2 * heads * group_count)
    used = 2 * heads * piece

    @pl.when(pl.program_id(0) == 0)
    def _():
        scale = row_norm(wide(hidden_ref[...]))
        scale_ref[...] = scale
        gains = jnp.zeros(gain_ref.shape, F32)
        for rel, small in enumerate(smalls):
            cut = chunk(index_ref, rel, depth)
            columns = wide(small[...]).T
            attn_ref[:, cut] = low(wide(hidden_ref[:, cut]) * scale * columns[0:1, :])
            moe_ref[:, cut] = columns[0:2, :]
            row = lax.broadcasted_iota(jnp.int32, (depth, gain_ref.shape[1]), 0)
            column = lax.broadcasted_iota(jnp.int32, (depth, gain_ref.shape[1]), 1)
            inside = column - (index_ref[0] ^ rel) * piece - (row // piece) * piece * group_count
            place = (inside == lax.rem(row, piece)) & (row < used)
            gains = gains + dot(low(columns), low(jnp.where(place, 1.0, 0.0)))[2:3, :]
        gain_ref[...] = gains

    total = jnp.zeros(out_ref.shape, F32)
    for rel, block in enumerate(blocks):
        total = total + dot(attn_ref[:, chunk(index_ref, rel, depth)], block[...])
    out_ref[...] = total
    square_ref[0] = jnp.sum(total * total, -1, keepdims=True)


def project(index, hidden, blocks, tile, heads):
    rows, width = hidden.shape
    depth = blocks[0].shape[0]
    count = len(blocks)
    if depth % 128:
        packed = place_rows(blocks, index)
        hidden = wide(hidden)
        scale = row_norm(hidden)
        attn_in = low(hidden * scale * wide(packed[:, 3 * tile]))
        projected = dot(attn_in, packed[:, : 3 * tile])
        squares = jnp.sum((projected * projected).reshape(rows, 3, tile), -1).T
        norm_gains = wide(packed[:, 3 * tile : 3 * tile + 2]).T
        gains = wide(packed[:, 3 * tile + 2]).reshape(count, depth)[:, : 2 * tile // count]
        gains = gains.reshape(count, 2, heads, -1).transpose(1, 2, 0, 3).reshape(2, tile)
        return attn_in, projected, squares, scale, norm_gains, gains
    attn_in, projected, squares, scale, norm_gains, gains = pl.pallas_call(
        functools.partial(project_kernel, count, heads),
        grid=(3,),
        out_shape=[
            jax.ShapeDtypeStruct((rows, width), BF16),
            jax.ShapeDtypeStruct((rows, 3 * tile), F32),
            jax.ShapeDtypeStruct((3, rows, 1), F32),
            jax.ShapeDtypeStruct((rows, 1), F32),
            jax.ShapeDtypeStruct((2, width), F32),
            jax.ShapeDtypeStruct((1, 2 * tile), F32),
        ],
        in_specs=[pl.BlockSpec(memory_space=pltpu.SMEM), whole_spec(hidden)]
        + [pl.BlockSpec((depth, 128), lambda i: (0, 3 * tile // 128))] * count
        + [column_spec(blocks[0], tile)] * count,
        out_specs=[
            whole_spec(hidden),
            pl.BlockSpec((rows, tile), lambda i: (0, i)),
            pl.BlockSpec((1, rows, 1), lambda i: (i, 0, 0)),
            pl.BlockSpec((rows, 1), lambda i: (0, 0)),
            pl.BlockSpec((2, width), lambda i: (0, 0)),
            pl.BlockSpec((1, 2 * tile), lambda i: (0, 0)),
        ],
        compiler_params=compiler_params(),
        cost_estimate=cost(12),
    )(index.reshape(1), hidden, *blocks, *blocks)
    return attn_in, projected, squares[:, :, 0], scale, norm_gains, gains.reshape(2, tile)


def swapped(values):
    half = values.shape[1] // 2
    return jnp.concatenate([values[:, half:], values[:, :half]], 1)


def turn_kernel(query_ref, key_ref, value_ref, scale_ref, gain_ref, cos_ref, sin_ref, *outs):
    query_out, pair_out = outs
    size = query_ref.shape[1]
    for part, (source, out_ref) in enumerate([(query_ref, query_out), (key_ref, pair_out)]):
        hat = source[...] * scale_ref[part] * gain_ref[part : part + 1, :]
        out_ref[:, :size] = low(hat * cos_ref[...] + swapped(hat) * sin_ref[...])
    pair_out[:, size:] = low(value_ref[...])


def turn_heads(projected, scales, gains, cosine, sine, heads):
    rows, size = cosine.shape
    return pl.pallas_call(
        turn_kernel,
        grid=(heads,),
        out_shape=[
            jax.ShapeDtypeStruct((rows, heads * size), BF16),
            jax.ShapeDtypeStruct((rows, 2 * heads * size), BF16),
        ],
        in_specs=[column_spec(projected, size, part * heads) for part in range(3)]
        + [whole_spec(scales), column_spec(gains, size), whole_spec(cosine), whole_spec(sine)],
        out_specs=[
            pl.BlockSpec((rows, size), lambda i: (0, i)),
            pl.BlockSpec((rows, 2 * size), lambda i: (0, i)),
        ],
        compiler_params=compiler_params(),
        cost_estimate=cost(6),
    )(projected, projected, projected, scales, gains, cosine, sine)


def turn_back_kernel(part_count, *refs):
    query_grad, parts = refs[0], refs[1 : 1 + part_count]
    query_ref, key_ref, scale_ref, gain_ref, cos_ref, sin_ref = refs[1 + part_count : 7 + part_count]
    query_out, key_out, value_out, inner_out, gain_out = refs[7 + part_count :]
    size = query_ref.shape[1]
    total = sum(wide(part[...]) for part in parts)
    value_out[...] = low(total[:, size:])
    pairs = [(query_grad[...], query_ref, query_out), (total[:, :size], key_ref, key_out)]
    for part, (grad, source, out_ref) in enumerate(pairs):
        hat = source[...] * scale_ref[part]
        norm_grad = grad * cos_ref[...] - swapped(grad) * sin_ref[...]
        gain_out[part : part + 1, :] = jnp.sum(norm_grad * hat, 0, keepdims=True)
        hat_grad = norm_grad * gain_ref[part : part + 1, :]
        out_ref[...] = hat_grad
        inner = jnp.sum(hat_grad * hat, -1, keepdims=True)

        @pl.when(pl.program_id(0) == 0)
        def _():
            inner_out[part] = inner

        @pl.when(pl.program_id(0) > 0)
        def _():
            inner_out[part] += inner


def turn_back(query_grad, parts, projected, scales, gains, cosine, sine, heads):
    rows, size = cosine.shape
    one = pl.BlockSpec((rows, size), lambda i: (0, i))
    two = pl.BlockSpec((rows, 2 * size), lambda i: (0, i))
    return pl.pallas_call(
        functools.partial(turn_back_kernel, len(parts)),
        grid=(heads,),
        out_shape=[jax.ShapeDtypeStruct((rows, heads * size), kind) for kind in (F32, F32, BF16)]
        + [
            jax.ShapeDtypeStruct((2, rows, 1), F32),
            jax.ShapeDtypeStruct((2, heads * size), F32),
        ],
        in_specs=[one]
        + [two] * len(parts)
        + [column_spec(projected, size, part * heads) for part in range(2)]
        + [whole_spec(scales), column_spec(gains, size), whole_spec(cosine), whole_spec(sine)],
        out_specs=[
            one,
            one,
            one,
            pl.BlockSpec((2, rows, 1), lambda i: (0, 0, 0)),
            pl.BlockSpec((2, size), lambda i: (0, i)),
        ],
        compiler_params=compiler_params(),
        cost_estimate=cost(8),
    )(query_grad, *parts, projected, projected, scales, gains, cosine, sine)


def input_grad_kernel(*refs):
    index_ref, query_grad, key_grad, value_low, projected, scale_ref, inner_ref = refs[:7]
    blocks, (low_ref, part_ref) = refs[7:-2], refs[-2:]
    size = query_grad.shape[1]
    depth = blocks[0].shape[0]
    for part, grad in enumerate([query_grad, key_grad]):
        cut = slice(part * size, (part + 1) * size)
        hat = projected[:, cut] * scale_ref[part]
        low_ref[:, cut] = low(scale_ref[part] * (grad[...] - hat * inner_ref[part]))
    low_ref[:, 2 * size :] = value_low[...]
    for rel, block in enumerate(blocks):
        part_ref[:, chunk(index_ref, rel, depth)] = low(dot(low_ref[...], block[...], 1, 1))


def input_grad(index, query_grad, key_grad, value_low, projected, scales, inner, blocks):
    rows, size = query_grad.shape
    depth = blocks[0].shape[0]
    if depth % 128:
        parts = []
        for part, grad in enumerate([query_grad, key_grad]):
            hat = projected[:, part * size : (part + 1) * size] * scales[part]
            parts.append(low(scales[part] * (grad - hat * inner[part])))
        qkv_low = jnp.concatenate(parts + [value_low], 1)
        return qkv_low, low(dot(qkv_low, place_rows(blocks, index)[:, : 3 * size], 1, 1))
    weights = pl.BlockSpec((depth, 3 * size), lambda i: (0, 0))
    values = [query_grad, key_grad, value_low, projected, scales, inner]
    return pl.pallas_call(
        input_grad_kernel,
        grid=(1,),
        out_shape=[
            jax.ShapeDtypeStruct((rows, 3 * size), BF16),
            jax.ShapeDtypeStruct((rows, depth * len(blocks)), BF16),
        ],
        in_specs=[pl.BlockSpec(memory_space=pltpu.SMEM)]
        + [whole_spec(value) for value in values]
        + [weights] * len(blocks),
        out_specs=[
            pl.BlockSpec((rows, 3 * size), lambda i: (0, 0)),
            pl.BlockSpec((rows, depth * len(blocks)), lambda i: (0, 0)),
        ],
        compiler_params=compiler_params(),
        cost_estimate=cost(12),
    )(index.reshape(1), *values, *blocks)


def route_kernel(tensor_count, expert_count, index_ref, tensor_ref, gain_ref, *refs):
    parts, routers = refs[:tensor_count], refs[tensor_count:-4]
    sent_ref, probs_ref, residual_ref, scale_ref = refs[-4:]
    quarter = parts[0].shape[1]
    rows, width = residual_ref.shape
    depth = routers[0].shape[0]
    for rel, part in enumerate(parts):
        residual_ref[:, chunk(tensor_ref, rel, quarter)] = part[...]
    residual = wide(residual_ref[...])
    scale = row_norm(residual)
    scale_ref[...] = scale
    sent_ref[:, :width] = low(residual * scale * gain_ref[...])
    logits = jnp.zeros((rows, routers[0].shape[1]), F32)
    for rel, router in enumerate(routers):
        logits = logits + dot(sent_ref[:, chunk(index_ref, rel, depth)], router[...])
    logits = logits[:, :expert_count]
    exponent = jnp.exp(logits - jnp.max(logits, -1, keepdims=True))
    probs = exponent / jnp.sum(exponent, -1, keepdims=True)
    probs_ref[...] = probs
    sent_ref[:, width:] = jnp.concatenate(split_low(probs), 1)


def route(index, tensor_index, gain, parts, blocks, cut, expert_count):
    rows, quarter = parts[0].shape
    width = quarter * len(parts)
    depth = blocks[0].shape[0]
    if depth % 128:
        residual = jnp.concatenate(in_order(parts, tensor_index), 1)
        scale = row_norm(wide(residual))
        moe_in = low(wide(residual) * scale * gain)
        logits = dot(moe_in, place_rows([plain(block)[:, cut] for block in blocks], index))
        logits = logits[:, :expert_count]
        exponent = jnp.exp(logits - jnp.max(logits, -1, keepdims=True))
        probs = exponent / jnp.sum(exponent, -1, keepdims=True)
        return jnp.concatenate([moe_in] + split_low(probs), 1), probs, residual, scale
    size = cut.stop - cut.start
    shapes = [(width + 2 * expert_count, BF16), (expert_count, F32), (width, BF16), (1, F32)]
    scalar = pl.BlockSpec(memory_space=pltpu.SMEM)
    return pl.pallas_call(
        functools.partial(route_kernel, len(parts), expert_count),
        grid=(1,),
        out_shape=[jax.ShapeDtypeStruct((rows, one), kind) for one, kind in shapes],
        in_specs=[scalar, scalar, whole_spec(gain)]
        + [whole_spec(part) for part in parts]
        + [block_spec(block, size, cut.start // size) for block in blocks],
        out_specs=[pl.BlockSpec((rows, one), lambda i: (0, 0)) for one, _ in shapes],
        compiler_params=compiler_params(),
        cost_estimate=cost(8),
    )(index.reshape(1), tensor_index.reshape(1), gain, *parts, *[array_of(b) for b in blocks])


def residual_kernel(tensor_count, group_count, index_ref, tensor_ref, *refs):
    gain_ref, logit_ref, residual_ref, scale_ref, grad_ref = refs[:5]
    parts, refs = refs[5 : 5 + tensor_count], refs[5 + tensor_count :]
    routers, blocks = refs[:group_count], refs[group_count : 2 * group_count]
    low_ref, share_ref, gain_out, heads_ref, scratch = refs[2 * group_count :]
    quarter = parts[0].shape[1]
    depth = blocks[0].shape[0]
    for rel, part in enumerate(parts):
        scratch[:, chunk(tensor_ref, rel, quarter)] = wide(part[...])
    for rel, router in enumerate(routers):
        scratch[:, chunk(index_ref, rel, depth)] += dot(logit_ref[...], router[...], 1, 1)
    normed = wide(residual_ref[...]) * scale_ref[...]
    gain_out[...] = jnp.sum(scratch[...] * normed, 0, keepdims=True)
    normed_grad = scratch[...] * gain_ref[...]
    mean = jnp.mean(normed_grad * normed, -1, keepdims=True)
    scratch[...] = wide(grad_ref[...]) + scale_ref[...] * (normed_grad - normed * mean)
    low_ref[...] = low(scratch[...])
    share_ref[...] = scratch[:, chunk(tensor_ref, 0, quarter)]
    total = jnp.zeros(heads_ref.shape, F32)
    for rel, block in enumerate(blocks):
        total = total + dot(low_ref[:, chunk(index_ref, rel, depth)], block[...])
    heads_ref[...] = low(total)


def residual_back(index, tensor_index, gain, logit, residual, scale, grad, parts, blocks, heads, cut):
    rows, quarter = parts[0].shape
    width = quarter * len(parts)
    depth = blocks[0].shape[0]
    if depth % 128:
        whole = place_rows([plain(block) for block in blocks], index)
        moe_in_grad = wide(jnp.concatenate(in_order(parts, tensor_index), 1))
        moe_in_grad = moe_in_grad + dot(logit, whole[:, cut], 1, 1)
        normed = wide(residual) * scale
        gain_grad = jnp.sum(moe_in_grad * normed, 0, keepdims=True)
        normed_grad = moe_in_grad * gain
        mean = jnp.mean(normed_grad * normed, -1, keepdims=True)
        total = wide(grad) + scale * (normed_grad - normed * mean)
        share = lax.dynamic_slice_in_dim(total, tensor_index * quarter, quarter, 1)
        return low(total), share, gain_grad, low(dot(low(total), whole[:, :heads]))
    size = cut.stop - cut.start
    shapes = [(rows, width, BF16), (rows, quarter, F32), (1, width, F32), (rows, heads, BF16)]
    scalar = pl.BlockSpec(memory_space=pltpu.SMEM)
    values = [gain, logit, residual, scale, grad] + parts
    arrays = [array_of(block) for block in blocks]
    return pl.pallas_call(
        functools.partial(residual_kernel, len(parts), len(blocks)),
        grid=(1,),
        out_shape=[jax.ShapeDtypeStruct((one, two), kind) for one, two, kind in shapes],
        in_specs=[scalar, scalar]
        + [whole_spec(value) for value in values]
        + [block_spec(block, size, cut.start // size) for block in blocks]
        + [block_spec(block, heads, 0) for block in blocks],
        out_specs=[pl.BlockSpec((one, two), lambda i: (0, 0)) for one, two, _ in shapes],
        scratch_shapes=[pltpu.VMEM((rows, width), F32)],
        compiler_params=compiler_params(),
        cost_estimate=cost(12),
    )(index.reshape(1), tensor_index.reshape(1), *values, *arrays, *arrays)


def late_dot_kernel(part_count, index_ref, *refs):
    traded, late = refs[:part_count], refs[part_count : 2 * part_count]
    blocks, (out_ref, router_ref) = refs[2 * part_count : -2], refs[-2:]
    tall, size = out_ref.shape
    total, router = jnp.zeros(out_ref.shape, F32), jnp.zeros(router_ref.shape, F32)
    for rel, block in enumerate(blocks):
        right = late[rel % part_count][rel // part_count]
        left = traded[rel % part_count][rel // part_count, :, :tall]
        total = total + dot(left, right[:, :size], 0, 0)
        router = router + dot(block[...], right[:, size:], 0, 0)
    out_ref[...] = total
    router_ref[...] = router


def late_dots(index, traded, late, blocks, tall, size):
    rows = blocks[0].shape[0]
    experts = late[0].shape[2] - size
    if size % 128:
        shard_count = traded[0].shape[0]
        left = jnp.concatenate([part[one] for one in range(shard_count) for part in traded])
        right = jnp.concatenate([part[one] for one in range(shard_count) for part in late])
        inputs = [lax.dynamic_slice_in_dim(block, index * size, size, 1) for block in blocks]
        out_grad = dot(left[:, :tall], right[:, :size], 0, 0)
        return out_grad, dot(jnp.concatenate(inputs), right[:, size:], 0, 0)
    return pl.pallas_call(
        functools.partial(late_dot_kernel, len(traded)),
        grid_spec=pltpu.PrefetchScalarGridSpec(
            num_scalar_prefetch=1,
            grid=(1,),
            in_specs=[pl.BlockSpec(one.shape, lambda i, s: (0, 0, 0)) for one in traded + late]
            + [pl.BlockSpec((rows, size), lambda i, s: (0, s[0]))] * len(blocks),
            out_specs=[
                pl.BlockSpec((tall, size), lambda i, s: (0, 0)),
                pl.BlockSpec((size, experts), lambda i, s: (0, 0)),
            ],
        ),
        out_shape=[
            jax.ShapeDtypeStruct((tall, size), F32),
            jax.ShapeDtypeStruct((size, experts), F32),
        ],
        compiler_params=compiler_params(),
        cost_estimate=cost(6),
    )(index.reshape(1), *traded, *late, *blocks)


def qkv_dot_kernel(part_count, first, *refs):
    traded, grads, outs = refs[:part_count], refs[part_count:-3], refs[-3:]
    size = outs[0].shape[1]
    for one, out_ref in enumerate(outs):
        total = jnp.zeros(out_ref.shape, F32)
        for rel, grad in enumerate(grads):
            left = traded[rel % part_count][rel // part_count, :, first:]
            total = total + dot(left, grad[:, one * size : (one + 1) * size], 0, 0)
        out_ref[...] = total


def qkv_dots(traded, grads, first, size):
    tall = traded[0].shape[2] - first
    if tall % 128:
        shard_count = traded[0].shape[0]
        left = jnp.concatenate([part[one] for one in range(shard_count) for part in traded])
        total = dot(left[:, first:], jnp.concatenate(grads), 0, 0)
        return [total[:, one * size : (one + 1) * size] for one in range(3)]
    return pl.pallas_call(
        functools.partial(qkv_dot_kernel, len(traded), first),
        grid=(1,),
        out_shape=[jax.ShapeDtypeStruct((tall, size), F32)] * 3,
        in_specs=[whole_spec(one) for one in traded + grads],
        out_specs=[pl.BlockSpec((tall, size), lambda i: (0, 0))] * 3,
        compiler_params=compiler_params(),
        cost_estimate=cost(8),
    )(*traded, *grads)


def per_device(
    tokens,
    parents,
    routes,
    pair_order,
    norm_attn,
    w_query,
    w_key,
    w_value,
    q_gain,
    k_gain,
    w_out,
    norm_moe,
    w_router,
    w_gate,
    w_up,
    w_down,
    out_grad,
):
    shard_index, context_index, tensor_index = (lax.axis_index(a) for a in (SH, CT, TS))
    context_count, tensor_count = lax.axis_size(CT), lax.axis_size(TS)
    group_count = lax.axis_size(SH) * context_count
    group = shard_index * context_count + context_index
    seg_dev, seg_len, quarter = tokens.shape[1:]
    rows = seg_dev * seg_len
    model_width = quarter * tensor_count
    slice_width = norm_attn.shape[0]
    top_count = routes.shape[3]
    expert_count = w_router.shape[1]
    expert_dev = w_gate.shape[0]
    local_heads, head_dim = q_gain.shape[0], q_gain.shape[1] * group_count
    head_width = local_heads * head_dim
    capacity = tensor_count * (
        (5 * rows * top_count + 4 * expert_count * tensor_count - 1)
        // (4 * expert_count * tensor_count)
    )
    score_scale = head_dim ** (-0.5)

    out_cut = slice(0, head_width)
    router_pad = -expert_count % 128
    router_cut = slice(head_width, head_width + expert_count + router_pad)
    gain_size = q_gain.size
    gain_values = jnp.concatenate([q_gain.reshape(-1), k_gain.reshape(-1)])
    gain_values = jnp.pad(gain_values, (0, slice_width - 2 * gain_size))
    base = 64
    order = jnp.arange(seg_dev, dtype=jnp.int32)[:, None] * (seg_len * top_count) + pair_order[0]
    order = order.reshape(rows, top_count)
    codes = jnp.concatenate([routes.reshape(rows, top_count), order // base, order % base], 1)
    codes = low(codes).reshape(slice_width, -1)
    columns = jnp.stack([norm_attn, norm_moe, gain_values], 1)
    columns = jnp.concatenate([columns, codes], 1)
    columns = jnp.pad(columns, ((0, 0), (0, 128 - columns.shape[1])))
    packed = jnp.concatenate([w_query, w_key, w_value, columns], 1)
    token_parts = around(hold(tokens.reshape(rows, quarter), packed), TS)
    grad_parts = double(hold(out_grad.reshape(1, rows, quarter), *token_parts[1:]), TS)
    qkv_blocks = gather_groups(packed, *token_parts[1:])
    hidden_in = jnp.concatenate(in_order(token_parts, tensor_index), 1)
    grad_output = jnp.concatenate(in_order(grad_parts, tensor_index), 1)

    first_code = 3 * head_width + 3
    codes = [block[:, first_code : first_code + codes.shape[1]] for block in qkv_blocks]
    codes = jnp.stack(codes).reshape(group_count, rows, 3, top_count).astype(jnp.int32)
    slots = own_slots(
        codes[:, :, 0],
        codes[:, :, 1] * base + codes[:, :, 2],
        group * expert_dev,
        expert_dev,
        capacity,
    )
    pad = -(-capacity // 16) * 16

    reachable, depths = tree_info(parents[0])
    first_slot = context_index * seg_dev
    local_depth = lax.dynamic_slice_in_dim(depths, first_slot, seg_dev, 0)
    offsets = jnp.arange(seg_len, dtype=jnp.int32)
    positions = (local_depth[:, None] * seg_len + offsets[None, :]).reshape(rows)
    cosine, sine = rope_tables(positions, head_dim)
    reach_local = lax.dynamic_slice_in_dim(reachable, first_slot, seg_dev, 0)
    masks = []
    for rel in range(context_count):
        other_slot = (context_index ^ rel) * seg_dev
        seen = lax.dynamic_slice_in_dim(reach_local, other_slot, seg_dev, 1)
        seen = seen[:, None, :, None]
        if rel == 0:
            same = jnp.eye(seg_dev, dtype=bool)[:, None, :, None]
            seen = seen & (~same | (offsets[None, :] <= offsets[:, None])[None, :, None, :])
        masks.append(jnp.broadcast_to(seen, (seg_dev, seg_len, seg_dev, seg_len)).reshape(rows, rows))
    bias = jnp.where(jnp.concatenate(masks, 1), 0.0, NEG_FILL)

    attn_in, projected, squares, scale_attn, norm_gains, gains = project(
        group, hidden_in, qkv_blocks, head_width, local_heads
    )
    gain_attn, gain_moe = norm_gains[0], norm_gains[1:]
    out_blocks = jnp.concatenate([w_out.T, jnp.pad(w_router, ((0, 0), (0, router_pad)))], 1)
    out_blocks = hold(out_blocks, qkv_blocks[context_count - 1])
    out_blocks = stack_far(gather_context(out_blocks, projected))
    squares = sum(around(squares[:2], TS))
    scales = lax.rsqrt(squares / model_width + EPS)[:, :, None]
    scales = hold(scales, grad_parts)
    query_rot, key_value = turn_heads(projected, scales, gains, cosine, sine, local_heads)
    key_value = gather_context(hold(key_value, *out_blocks[1:context_count]))
    query_rot = hold(query_rot, slots)
    attended_low, log_total = attend(query_rot, key_value, bias, head_dim)

    def tensor_parts(value):
        return [
            lax.dynamic_slice_in_dim(value, (tensor_index ^ rel) * quarter, quarter, 1)
            for rel in range(tensor_count)
        ]

    def tensor_sum(parts):
        total = wide(parts[0])
        for rel in range(1, tensor_count):
            total = total + wide(swap(low(parts[rel]), TS, rel))
        return total

    attn_part = scatter_dot(group, attended_low, out_blocks, out_cut, F32)
    attn_share = tensor_sum(tensor_parts(attn_part))
    residual_share = wide(tokens.reshape(rows, quarter)) + attn_share
    grad_blocks = gather_context(hold(grad_output, *key_value[1:]), residual_share)
    parts = around(low(residual_share), TS)
    parts[-1] = hold(parts[-1], grad_blocks[-1])
    sent, router_probs, residual, scale_moe = route(
        group, tensor_index, gain_moe, parts, out_blocks, router_cut, expert_count
    )
    moe_in = sent[:, :model_width]
    grad_blocks = stack_far(grad_blocks[:-1] + [hold(grad_blocks[-1], sent)])
    grad_rows = dispatch(slots, grad_blocks, pad)
    blocks = gather_groups(sent, grad_rows)
    grad_rows = grad_rows.reshape(expert_dev, group_count * pad, model_width)

    def slices(value):
        return [
            lax.dynamic_slice_in_dim(value, (group ^ rel) * slice_width, slice_width, 1)
            for rel in range(group_count)
        ]

    late = hold(jnp.concatenate([attended_low, attn_in], 1), blocks[1])
    traded = [jnp.concatenate([late[:, :head_width], one], 1) for one in slices(late[:, head_width:])]
    traded = trade_start(jnp.stack(traded), blocks[-1])
    first = (group * expert_dev).reshape(1)
    pair_rows, act_gated, pair_back, *row_parts = experts(
        first,
        slots,
        blocks,
        grad_rows,
        w_gate,
        w_up,
        w_down,
        pad,
        expert_count,
    )
    row_far = joint(row_parts[context_count:], *traded[1:])
    row_own = core_sum(row_far, row_parts[:context_count])
    row_came = context_start(row_own)
    *mixed_near, mixed_far = expert_out(
        slots, act_gated, w_down, pad, context_count, *[block[1] for block in row_own[1:]]
    )
    row_total = context_end(row_own, row_came, mixed_near[0])
    (down_grad,) = weight_grad(act_gated, grad_rows, 1, row_total)
    mixed_far = swap(mixed_far, SH, 1)
    (down_grad,) = weight_grad(act_gated, grad_rows, 1, row_total)

    row_low = low(row_total)
    parts = [
        jnp.concatenate([part, row_low[:, model_width:]], 1)
        for part in tensor_parts(row_low[:, :model_width])
    ]
    parts = [parts[0]] + [swap(parts[rel], TS, rel) for rel in range(1, tensor_count)]
    parts[-1] = hold(parts[-1], down_grad, mixed_far)
    row_share = sum(wide(part[:, :quarter]) for part in parts)
    gate_w_grad, up_w_grad = weight_grad(pair_rows, pair_back, 2, row_share)
    prob_grads = sum(wide(part[:, quarter:]) for part in in_order(parts, tensor_index))
    prob_grads = prob_grads[:, :expert_count] + prob_grads[:, expert_count:]
    logit_low = low(
        router_probs * (prob_grads - jnp.sum(prob_grads * router_probs, -1, keepdims=True))
    )
    mixed_far = hold(mixed_far, row_share)
    mixed_own = [(block, mixed_far[one]) for one, block in enumerate(mixed_near)]
    mixed_came = context_start(mixed_own)
    parts = around(low(row_share), TS)
    parts[-1] = hold(parts[-1], gate_w_grad, *mixed_came)
    logit_wide = jnp.pad(logit_low, ((0, 0), (0, router_pad)))
    residual_low, residual_share_grad, gain_moe_grad, grad_heads = residual_back(
        group,
        tensor_index,
        gain_moe,
        logit_wide,
        residual,
        scale_moe,
        grad_output,
        parts,
        out_blocks,
        head_width,
        router_cut,
    )
    mixed_total = context_end(mixed_own, mixed_came, gate_w_grad)
    query_grad, *key_value_grad = attend_back(
        query_rot, grad_heads, log_total, key_value, bias, head_dim
    )
    key_value_grad[-1] = hold(key_value_grad[-1], mixed_total)
    traded_late = [jnp.concatenate([one, logit_low], 1) for one in slices(residual_low)]
    key_value_grad = [(block,) for block in key_value_grad]
    key_value_grad = context_end(key_value_grad, context_start(key_value_grad))
    traded_late = trade_start(jnp.stack(traded_late), key_value_grad)
    key_value_grad = [key_value_grad]
    query_hat_grad, key_hat_grad, value_low, inner, gain_grads = turn_back(
        query_grad, key_value_grad, projected, scales, gains, cosine, sine, local_heads
    )
    inner = butterfly(inner[:, :, 0], TS)[:, :, None] / model_width
    inner = hold(inner, *traded_late[1:])
    qkv_low, attn_part = input_grad(
        group, query_hat_grad, key_hat_grad, value_low, projected, scales, inner, qkv_blocks
    )
    traded_late[0] = hold(traded_late[0], qkv_low)
    out_w_grad, router_grad = late_dots(
        group, traded, traded_late, blocks, head_width, slice_width
    )
    qkv_grads = gather_groups(qkv_low)
    attn_share = tensor_sum(tensor_parts(attn_part))
    attn_share = hold(attn_share, *qkv_grads[1:context_count])
    hidden_share = wide(tokens.reshape(rows, quarter))
    normed_share = hidden_share * scale_attn
    normed_in_grad = attn_share * lax.dynamic_slice_in_dim(gain_attn, tensor_index * quarter, quarter)
    inner = jnp.sum(normed_in_grad * normed_share, -1)
    ends = jnp.zeros((rows + model_width,), F32)
    ends = lax.dynamic_update_slice_in_dim(
        ends, jnp.sum(attn_share * normed_share, 0), rows + tensor_index * quarter, 0
    )
    ends = butterfly(lax.dynamic_update_slice_in_dim(ends, inner, 0, 0), TS)
    inner = ends[:rows, None] / model_width
    gain_attn_grad = ends[rows:]
    mixed_share = tensor_sum(tensor_parts(hold(mixed_total, attn_share)))
    mixed_out = low(residual_share + mixed_share).reshape(tokens.shape)
    traded[0] = hold(traded[0], out_w_grad, mixed_share)
    qkv_w_grads = qkv_dots(traded, qkv_grads, head_width, head_width)
    tokens_grad = residual_share_grad + scale_attn * (normed_in_grad - normed_share * inner)

    gain_grads = gain_grads.reshape(2, local_heads, group_count, -1)
    gain_grads = gain_grads.transpose(2, 0, 1, 3).reshape(group_count, 2 * gain_size)
    vectors = jnp.concatenate(
        [
            gain_attn_grad.reshape(group_count, slice_width),
            gain_moe_grad.reshape(group_count, slice_width),
            gain_grads,
        ],
        1,
    )
    vectors = jnp.concatenate(
        [
            lax.dynamic_slice_in_dim(vectors, group ^ rel, 1, 0)[:, None]
            for rel in range(group_count)
        ]
    )
    vectors = core_sum([vectors[context_count:]], [vectors[:context_count]])
    vectors = add_up(vectors[0])
    vectors = vectors[0] + sum(swap(vectors[rel], CT, rel) for rel in range(1, context_count))
    vectors = vectors[0]
    gain_grads = vectors[2 * slice_width :].reshape((2,) + q_gain.shape)
    return (
        mixed_out,
        tokens_grad.reshape(tokens.shape),
        vectors[:slice_width],
        *qkv_w_grads,
        gain_grads[0],
        gain_grads[1],
        out_w_grad,
        vectors[slice_width : 2 * slice_width],
        router_grad,
        gate_w_grad,
        up_w_grad,
        down_grad,
    )


def solution(mesh):
    both = (SH, CT)
    rows = P(SH, CT, None, TS)
    pairs = P(SH, CT, None, None)
    vector, matrix, turned = P(both), P(both, TS), P(TS, both)
    up, down = P(both, None, TS), P(both, TS, None)
    return jax.shard_map(
        per_device,
        mesh=mesh,
        in_specs=(
            rows,
            P(SH, None),
            pairs,
            P(SH, CT, None),
            vector,
            matrix,
            matrix,
            matrix,
            turned,
            turned,
            turned,
            vector,
            P(both, None),
            up,
            up,
            down,
            rows,
        ),
        out_specs=(
            rows,
            rows,
            vector,
            matrix,
            matrix,
            matrix,
            turned,
            turned,
            turned,
            vector,
            P(both, None),
            up,
            up,
            down,
        ),
        check_vma=False,
    )
```

time: 951 us -> 599 us (0.63)
  matrix products: 213 us -> 0 us
  waiting for transfers between devices: 363 us -> 159 us
  Pallas kernels: 0 us -> 171 us
  local copies, waits for them, and re-layouts: 196 us -> 86.7 us
    dot_general x50 -> x0, matrix products: 213 us -> none  [the longest x9 119 us: by_expert(): return jnp.einsum(spec, left, right, preferred_element_type=F32)]
    ppermute x115 -> x97, waiting for transfers between devices: 363 us -> 159 us  [swap(): return lax.ppermute(value, axis, [(i, i ^ rel) for i in range(count)])]
    pallas_call x0 -> x59, Pallas kernels: none -> 171 us  [the longest x1 47.1 us: experts(): pl.pallas_call(functools.partial(experts_kernel, group_count, pad, pieces...]
    dynamic_update_slice x36 -> x2, local copies, waits for them, and re-layouts: 51.1 us -> 0.55 us  [the longest x1 0.55 us: per_device(): lax.dynamic_update_slice_in_dim(ends, jnp.sum(attn_share * normed_share,...]
    concatenate x12 -> x14, local copies, waits for them, and re-layouts: 27.2 us -> 0.81 us  [the longest x2 0.44 us: per_device(): columns = jnp.concatenate([columns, codes], 1)]
    another operation x10 -> x20, other arithmetic: 2.82 us -> 13.5 us  [the longest x10 7.77 us: context_start(): return [swap(jnp.stack(upper), CT, 1), swap(jnp.stack(lower), CT, 2)]]
    reshape x9 -> x5, local copies, waits for them, and re-layouts: 11.2 us -> 0.86 us  [the longest x1 0.6 us: project(): gains.reshape(2, tile)]
    convert_element_type x3 -> x1, other arithmetic: 10.3 us -> 0.04 us  [per_device(): jnp.stack(codes).reshape(group_count, rows, 3, top_count).astype(jnp.int32)]
  transfers between devices with their start and end apart: 115 -> 97, of which waited for: 50 -> 40; matrix products, arithmetic and copies ran while one was open for 44% -> 17% of each run, Pallas kernels for 0% -> 26%
where the time goes in v1:
time: 599 us; the launch traced here: 588 us
  Pallas kernels  171 us (29%)
  waiting for transfers between devices  159 us (27%)
  starting transfers between devices  102 us (17%)
  local copies, waits for them, and re-layouts  86.7 us (14%)
  other arithmetic  66.2 us (11%)
    ppermute x97, waiting for transfers between devices, swap(): return lax.ppermute(value, axis, [(i, i ^ rel) for i in range(count)])  159 us
    ppermute x97, starting transfers between devices, swap(): return lax.ppermute(value, axis, [(i, i ^ rel) for i in range(count)])  102 us
    pallas_call x1, Pallas kernels, experts(): pl.pallas_call(functools.partial(experts_kernel, group_count, pad, pieces...  47.1 us
    unnamed x233, local copies, waits for them, and re-layouts  41.9 us
    pallas_call x2, Pallas kernels, weight_grad(): pl.pallas_call(functools.partial(weight_grad_kernel, pieces, len(earlier)...  35.2 us
    pallas_call x1, Pallas kernels, expert_out(): pl.pallas_call(functools.partial(expert_out_kernel, pad, pieces, len(earl...  17.3 us
  transfers between devices with their start and end apart: 97, of which 40 were waited for; matrix products, arithmetic and copies ran while one was open for 17% of the time, Pallas kernels for 26%

profile of v1, /device:TPU:8, one launch (start us, length us, event | category | flops | bytes accessed | tf_op | source)
XLA Modules:
  0.0 588.1 jit_solution(8934692338912935761)
XLA Ops:
  57.4 7.4 %collective-permute-done.15 = bf16[2,256,512]{2,1,0:T(8,128)(2,1)S(1)} collective-permute-done((bf16[2,256,512]{2,1,0:T(8,128)(2,1)}, bf16[2,256,512]{2,1,0:T(8,128)(2,1)S(1)}, u32[]{:S(2)}, u32[]{:S(2)}) %collective-permute-start.15) | collective-permute-done | bytes 524320 | tf_op jit(solution)/shard_map/ppermute | solution.py:21
  77.3 7.6 %shard_map.275 = (bf16[256,2048]{1,0:T(8,128)(2,1)}, f32[256,1536]{1,0:T(8,128)}, f32[3,256,1]{2,1,0:T(8,128)}, f32[256,1]{1,0:T(8,128)}, f32[2,2048]{1,0:T(2,128)}, /*index=5*/f32[1,1024]{1,0:T(1,128)}) custom-call(s32[1]{0:T(128)} %bitcast.1.index_ref.refs_0_, bf16[256,2048]{1,0:T(8,128)(2,1)} %pad_maximum_fusion.8.hidden_ref, ...), custom_call_target="tpu_custom_call" | custom-call | flops 12000000000 | tf_op jit(solution)/shard_map/pallas_call | solution.py:737
  107.0 5.1 convert_reduce_fusion
  127.8 6.0 %shard_map.284 = (bf16[256,512]{1,0:T(8,128)(2,1)}, f32[4,256,1]{2,1,0:T(8,128)}) custom-call(bf16[256,512]{1,0:T(8,128)(2,1)} %shard_map.279.query_ref, f32[256,1024]{1,0:T(8,128)} %add_select_fusion.bias_ref, bf16[256,1024]{1,0:T(8,128)(2,1)} %shard_map.283.refs_0_, bf16[256,1024]{1,0:T(8,128)(2,1)} %copy-done.53, bf16[256,1024]{1,0:T(8,128)(2,1)} %copy-done.54, ...), custom_call_target="tpu_custom_call" | custom-call | flops 12000000000 | tf_op jit(solution)/shard_map/pallas_call | solution.py:616
  143.8 7.3 %collective-permute-done.25 = bf16[256,512]{1,0:T(8,128)(2,1)S(1)} collective-permute-done((bf16[256,512]{1,0:T(8,128)(2,1)}, bf16[256,512]{1,0:T(8,128)(2,1)S(1)}, u32[]{:S(2)}, u32[]{:S(2)}) %collective-permute-start.25) | collective-permute-done | bytes 262176 | tf_op jit(solution)/shard_map/ppermute | solution.py:21
  151.0 8.5 %collective-permute-done.26 = bf16[256,512]{1,0:T(8,128)(2,1)S(1)} collective-permute-done((bf16[256,512]{1,0:T(8,128)(2,1)S(1)}, bf16[256,512]{1,0:T(8,128)(2,1)S(1)}, u32[]{:S(2)}, u32[]{:S(2)}) %collective-permute-start.26) | collective-permute-done | bytes 262176 | tf_op jit(solution)/shard_map/ppermute | solution.py:21
  181.5 7.0 %collective-permute-done.34.refs_0_ = bf16[256,512]{1,0:T(8,128)(2,1)S(1)} collective-permute-done((bf16[256,512]{1,0:T(8,128)(2,1)}, bf16[256,512]{1,0:T(8,128)(2,1)S(1)}, u32[]{:S(2)}, u32[]{:S(2)}) %collective-permute-start.34) | collective-permute-done | bytes 262176 | tf_op jit(solution)/shard_map/ppermute | solution.py:21
  208.0 9.9 %shard_map.292.refs_1_ = bf16[8,8,48,2048]{3,2,1,0:T(8,128)(2,1)} custom-call(s32[8,8,256]{2,1,0:T(8,128)} %fusion.86.refs_1_.slots_ref, bf16[256,2048]{1,0:T(8,128)(2,1)} %shard_map.286.refs_0_, bf16[256,2048]{1,0:T(8,128)(2,1)} %shard_map.287.refs_1_, bf16[256,2048]{1,0:T(8,128)(2,1)} %shard_map.288.refs_2_, bf16[256,2048]{1,0:T(8,128)(2,1)} %shard_map.291.refs_3_, ...), custom_call_target="tpu_custom_call" | custom-call | flops 12000000000 | tf_op jit(solution)/shard_map/pallas_call | solution.py:290
  217.9 9.8 %collective-permute-done.36.refs_0_ = bf16[256,2176]{1,0:T(8,128)(2,1)S(1)} collective-permute-done((bf16[256,2176]{1,0:T(8,128)(2,1)}, bf16[256,2176]{1,0:T(8,128)(2,1)S(1)}, u32[]{:S(2)}, u32[]{:S(2)}) %collective-permute-start.36) | collective-permute-done | bytes 1114144 | tf_op jit(solution)/shard_map/ppermute | solution.py:21
  239.6 5.7 collective-permute-done.38
  259.5 47.1 %shard_map.295 = (bf16[8,384,2048]{2,1,0:T(8,128)(2,1)}, bf16[8,384,256]{2,1,0:T(8,128)(2,1)}, bf16[8,384,512]{2,1,0:T(8,128)(2,1)}, bf16[256,2176]{1,0:T(8,128)...) custom-call(s32[1]{0:T(128)} %bitcast.30.first_ref, ...), custom_call_target="tpu_custom_call" | custom-call | flops 99999997952 | tf_op jit(solution)/shard_map/pallas_call | solution.py:436
  318.5 17.3 %shard_map.304 = (bf16[256,2048]{1,0:T(8,128)(2,1)}, bf16[256,2048]{1,0:T(8,128)(2,1)}, bf16[256,2048]{1,0:T(8,128)(2,1)}, bf16[256,2048]{1,0:T(8,128)(2,1)}, bf16[4,256,2048]{2,1,0:T(8,128)(2,1)}) custom-call(s32[8,8,256]{2,1,0:T(8,128)} %fusion.86.refs_1_.slots_ref, bf16[8,384,256]{2,1,0:T(8,128)(2,1)} %get-tuple-element.75.act_ref.left_ref, ...), custom_call_target="tpu_custom_call" | custom-call | flops 40000000000 | tf_op jit(solution)/shard_map/pallas_call | solution.py:483
  335.9 5.6 collective-permute-done.54.refs_1_.refs_0_
  350.8 10.6 %collective-permute-done.56 = bf16[128,2176]{1,0:T(8,128)(2,1)S(1)} collective-permute-done((bf16[128,2176]{1,0:T(8,128)(2,1)S(1)}, bf16[128,2176]{1,0:T(8,128)(2,1)S(1)}, u32[]{:S(2)}, u32[]{:S(2)}) %collective-permute-start.56) | collective-permute-done | bytes 557088 | tf_op jit(solution)/shard_map/ppermute | solution.py:21
  372.0 15.2 %shard_map.307.refs_1_ = f32[8,256,2048]{2,1,0:T(8,128)} custom-call(bf16[8,384,256]{2,1,0:T(8,128)(2,1)} %get-tuple-element.75.act_ref.left_ref, bf16[8,384,2048]{2,1,0:T(8,128)(2,1)} %bitcast.323, f32[256,2176]{1,0:T(8,128)} %pad_maximum_fusion.1.outs_0_), custom_call_target="tpu_custom_call" | custom-call | flops 80000000000 | tf_op jit(solution)/shard_map/pallas_call | solution.py:546
  388.2 5.8 collective-permute-done.58
  408.1 19.9 %shard_map.310 = (f32[8,2048,256]{2,1,0:T(8,128)}, f32[8,2048,256]{2,1,0:T(8,128)}) custom-call(bf16[8,384,2048]{2,1,0:T(8,128)(2,1)} %get-tuple-element.90.left_ref, bf16[8,384,512]{2,1,0:T(8,128)(2,1)} %get-tuple-element.91.right_ref, f32[256,512]{1,0:T(8,128)} %get-tuple-element.211.refs_1_.outs_0_), custom_call_target="tpu_custom_call" | custom-call | flops 80000000000 | tf_op jit(solution)/shard_map/pallas_call | solution.py:546
  436.9 5.7 shard_map.314
  442.6 7.5 %shard_map.315 = (f32[256,512]{1,0:T(8,128)}, bf16[256,1024]{1,0:T(8,128)(2,1)}, bf16[256,1024]{1,0:T(8,128)(2,1)}, bf16[256,1024]{1,0:T(8,128)(2,1)}, bf16[256,1024]{1,0:T(8,128)(2,1)}) custom-call(bf16[256,512]{1,0:T(8,128)(2,1)} %shard_map.279.query_ref, bf16[256,512]{1,0:T(8,128)(2,1)} %get-tuple-element.96.grad_ref, ...), custom_call_target="tpu_custom_call" | custom-call | flops 12000000000 | tf_op jit(solution)/shard_map/pallas_call | solution.py:657
  461.3 5.7 collective-permute-done.68.refs_1_.refs_0_
  478.7 6.6 %collective-permute-done.69 = bf16[128,1024]{1,0:T(8,128)(2,1)} collective-permute-done((bf16[128,1024]{1,0:T(8,128)(2,1)}, bf16[128,1024]{1,0:T(8,128)(2,1)}, u32[]{:S(2)}, u32[]{:S(2)}) %collective-permute-start.69) | collective-permute-done | bytes 262176 | tf_op jit(solution)/shard_map/ppermute | solution.py:21
  508.7 6.7 %shard_map.324 = (bf16[256,1536]{1,0:T(8,128)(2,1)}, bf16[256,2048]{1,0:T(8,128)(2,1)}) custom-call(s32[1]{0:T(128)} %bitcast.1.index_ref.refs_0_, f32[256,512]{1,0:T(8,128)} %get-tuple-element.103.refs_1_, f32[256,512]{1,0:T(8,128)} %get-tuple-element.104.refs_2_, bf16[256,512]{1,0:T(8,128)(2,1)} %get-tuple-element.105.refs_3_, ...), custom_call_target="tpu_custom_call" | custom-call | flops 12000000000 | tf_op jit(solution)/shard_map/pallas_call | solution.py:878
  567.8 11.2 %collective-permute-done.86 = bf16[256,512]{1,0:T(8,128)(2,1)S(1)} collective-permute-done((bf16[256,512]{1,0:T(8,128)(2,1)}, bf16[256,512]{1,0:T(8,128)(2,1)S(1)}, u32[]{:S(2)}, u32[]{:S(2)}) %collective-permute-start.86) | collective-permute-done | bytes 262176 | tf_op jit(solution)/shard_map/ppermute | solution.py:21
  581.3 6.4 %shard_map.330 = (f32[256,512]{1,0:T(8,128)}, f32[256,512]{1,0:T(8,128)}, f32[256,512]{1,0:T(8,128)}) custom-call(bf16[2,256,768]{2,1,0:T(8,128)(2,1)} %shard_map.329.refs_0_, bf16[2,256,768]{2,1,0:T(8,128)(2,1)} %collective-permute-done.45.refs_4_.refs_1_, bf16[2,256,768]{2,1,0:T(8,128)(2,1)} %collective-permute-done.46.refs_5_.refs_2_, ...), custom_call_target="tpu_custom_call" | custom-call | flops 8000000000 | tf_op jit(solution)/shard_map/pallas_call | solution.py:1070
  (646 shorter events, 338.8 us)
Async XLA Ops:
  8.8 22.7 %collective-permute-start.1 = (bf16[256,512]{1,0:T(8,128)(2,1)}, bf16[256,512]{1,0:T(8,128)(2,1)S(1)}, u32[]{:S(2)}, u32[]{:S(2)}) collective-permute-start(bf16[256,512]{1,0:T(8,128)(2,1)} %shard_map.272), channel_id=1, source_target_pairs={{0,2},{1,3},{2,0},{3,1},{4,6},{5,7},{6,4},{7,5},{8,10},{9,11},{10,... | collective-permute-start | bytes 786440 | tf_op jit(solution)/shard_map/ppermute | solution.py:21
  11.3 33.6 %collective-permute-start.4 = (bf16[256,1664]{1,0:T(8,128)(2,1)S(1)}, bf16[256,1664]{1,0:T(8,128)(2,1)}, u32[]{:S(2)}, u32[]{:S(2)}) collective-permute-start(bf16[256,1664]{1,0:T(8,128)(2,1)S(1)} %copy-done.36), channel_id=1, source_target_pairs={{0,8},{4,12},{8,0},{12,4},{1,9},{5,13},{9,1},{13,5},{2,10},{6,14},... | collective-permute-start | bytes 2555912 | tf_op jit(solution)/shard_map/ppermute | solution.py:21
  12.8 33.9 %collective-permute-start.3 = (bf16[256,1664]{1,0:T(8,128)(2,1)S(1)}, bf16[256,1664]{1,0:T(8,128)(2,1)S(1)}, u32[]{:S(2)}, u32[]{:S(2)}) collective-permute-start(bf16[256,1664]{1,0:T(8,128)(2,1)S(1)} %copy-done.36), channel_id=1, source_target_pairs={{0,4},{4,0},{8,12},{12,8},{1,5},{5,1},{9,13},{13,9},{2,6},{6,2},{1... | collective-permute-start | bytes 2555912 | tf_op jit(solution)/shard_map/ppermute | solution.py:21
  27.7 25.8 %collective-permute-start.7 = (bf16[256,1664]{1,0:T(8,128)(2,1)S(1)}, bf16[256,1664]{1,0:T(8,128)(2,1)}, u32[]{:S(2)}, u32[]{:S(2)}) collective-permute-start(bf16[256,1664]{1,0:T(8,128)(2,1)S(1)} %copy-done.36), channel_id=1, source_target_pairs={{0,16},{16,0},{1,17},{17,1},{2,18},{18,2},{3,19},{19,3},{4,20},{20... | collective-permute-start | bytes 2555912 | tf_op jit(solution)/shard_map/ppermute | solution.py:21
  41.4 23.4 %collective-permute-start.15 = (bf16[2,256,512]{2,1,0:T(8,128)(2,1)}, bf16[2,256,512]{2,1,0:T(8,128)(2,1)S(1)}, u32[]{:S(2)}, u32[]{:S(2)}) collective-permute-start(bf16[2,256,512]{2,1,0:T(8,128)(2,1)} %pad_maximum_fusion.27), channel_id=1, source_target_pairs={{0,2},{1,3},{2,0},{3,1},{4,6},{5,7},{6,4},{7,5},{8,10},{9,11},{10,... | collective-permute-start | bytes 1572872 | tf_op jit(solution)/shard_map/ppermute | solution.py:21
  46.8 28.6 %collective-permute-start.9 = (bf16[256,1664]{1,0:T(8,128)(2,1)}, bf16[256,1664]{1,0:T(8,128)(2,1)}, u32[]{:S(2)}, u32[]{:S(2)}) collective-permute-start(bf16[256,1664]{1,0:T(8,128)(2,1)} %shard_map.274.refs_2_.refs_10_.refs_9_), channel_id=1, source_target_pairs={{0,16},{16,0},{1,17},{17,1},{2,18},{18,2},{3,19},{19,3},{4,20},{20... | collective-permute-start | bytes 2555912 | tf_op jit(solution)/shard_map/ppermute | solution.py:21
  49.5 24.8 %collective-permute-start.8 = (bf16[256,1664]{1,0:T(8,128)(2,1)}, bf16[256,1664]{1,0:T(8,128)(2,1)}, u32[]{:S(2)}, u32[]{:S(2)}) collective-permute-start(bf16[256,1664]{1,0:T(8,128)(2,1)} %shard_map.273.refs_1_.refs_9_.refs_8_), channel_id=1, source_target_pairs={{0,16},{16,0},{1,17},{17,1},{2,18},{18,2},{3,19},{19,3},{4,20},{20... | collective-permute-start | bytes 2555912 | tf_op jit(solution)/shard_map/ppermute | solution.py:21
  126.0 42.7 %collective-permute-start.29 = (bf16[256,2048]{1,0:T(8,128)(2,1)}, bf16[256,2048]{1,0:T(8,128)(2,1)S(1)}, u32[]{:S(2)}, u32[]{:S(2)}) collective-permute-start(bf16[256,2048]{1,0:T(8,128)(2,1)} %shard_map.286.refs_0_), channel_id=1, source_target_pairs={{0,8},{4,12},{8,0},{12,4},{1,9},{5,13},{9,1},{13,5},{2,10},{6,14},... | collective-permute-start | bytes 3145736 | tf_op jit(solution)/shard_map/ppermute | solution.py:21
  127.5 38.5 %collective-permute-start.28 = (bf16[256,2048]{1,0:T(8,128)(2,1)}, bf16[256,2048]{1,0:T(8,128)(2,1)S(1)}, u32[]{:S(2)}, u32[]{:S(2)}) collective-permute-start(bf16[256,2048]{1,0:T(8,128)(2,1)} %shard_map.286.refs_0_), channel_id=1, source_target_pairs={{0,4},{4,0},{8,12},{12,8},{1,5},{5,1},{9,13},{13,9},{2,6},{6,2},{1... | collective-permute-start | bytes 3145736 | tf_op jit(solution)/shard_map/ppermute | solution.py:21
  200.5 27.2 %collective-permute-start.36 = (bf16[256,2176]{1,0:T(8,128)(2,1)}, bf16[256,2176]{1,0:T(8,128)(2,1)S(1)}, u32[]{:S(2)}, u32[]{:S(2)}) collective-permute-start(bf16[256,2176]{1,0:T(8,128)(2,1)} %get-tuple-element.74.refs_1_.refs_0_.refs_8_), channel_id=1, source_target_pairs={{0,4},{4,0},{8,12},{12,8},{1,5},{5,1},{9,13},{13,9},{2,6},{6,2},{1... | collective-permute-start | bytes 3342344 | tf_op jit(solution)/shard_map/ppermute | solution.py:21
  201.6 33.5 %collective-permute-start.37 = (bf16[256,2176]{1,0:T(8,128)(2,1)}, bf16[256,2176]{1,0:T(8,128)(2,1)S(1)}, u32[]{:S(2)}, u32[]{:S(2)}) collective-permute-start(bf16[256,2176]{1,0:T(8,128)(2,1)} %get-tuple-element.74.refs_1_.refs_0_.refs_8_), channel_id=1, source_target_pairs={{0,8},{4,12},{8,0},{12,4},{1,9},{5,13},{9,1},{13,5},{2,10},{6,14},... | collective-permute-start | bytes 3342344 | tf_op jit(solution)/shard_map/ppermute | solution.py:21
  256.0 50.6 %collective-permute-start.47 = (bf16[2,256,768]{2,1,0:T(8,128)(2,1)}, bf16[2,256,768]{2,1,0:T(8,128)(2,1)S(1)}, u32[]{:S(2)}, u32[]{:S(2)}) collective-permute-start(bf16[2,256,768]{2,1,0:T(8,128)(2,1)} %shard_map.299), channel_id=1, source_target_pairs={{0,12},{4,8},{8,4},{12,0},{1,13},{5,9},{9,5},{13,1},{2,14},{6,10},... | collective-permute-start | bytes 2359304 | tf_op jit(solution)/shard_map/ppermute | solution.py:21
  257.6 49.0 %collective-permute-start.46 = (bf16[2,256,768]{2,1,0:T(8,128)(2,1)}, bf16[2,256,768]{2,1,0:T(8,128)(2,1)}, u32[]{:S(2)}, u32[]{:S(2)}) collective-permute-start(bf16[2,256,768]{2,1,0:T(8,128)(2,1)} %shard_map.298), channel_id=1, source_target_pairs={{0,8},{4,12},{8,0},{12,4},{1,9},{5,13},{9,1},{13,5},{2,10},{6,14},... | collective-permute-start | bytes 2359304 | tf_op jit(solution)/shard_map/ppermute | solution.py:21
  259.2 47.5 %collective-permute-start.45 = (bf16[2,256,768]{2,1,0:T(8,128)(2,1)}, bf16[2,256,768]{2,1,0:T(8,128)(2,1)}, u32[]{:S(2)}, u32[]{:S(2)}) collective-permute-start(bf16[2,256,768]{2,1,0:T(8,128)(2,1)} %shard_map.297), channel_id=1, source_target_pairs={{0,4},{4,0},{8,12},{12,8},{1,5},{5,1},{9,13},{13,9},{2,6},{6,2},{1... | collective-permute-start | bytes 2359304 | tf_op jit(solution)/shard_map/ppermute | solution.py:21
  308.8 42.0 %collective-permute-start.52 = (bf16[256,2176]{1,0:T(8,128)(2,1)S(1)}, bf16[256,2176]{1,0:T(8,128)(2,1)}, u32[]{:S(2)}, u32[]{:S(2)}) collective-permute-start(bf16[256,2176]{1,0:T(8,128)(2,1)S(1)} %copy-done), channel_id=1, source_target_pairs={{0,16},{16,0},{1,17},{17,1},{2,18},{18,2},{3,19},{19,3},{4,20},{20... | collective-permute-start | bytes 3342344 | tf_op jit(solution)/shard_map/ppermute | solution.py:21
  314.8 26.7 %collective-permute-start.54 = (bf16[2,128,2176]{2,1,0:T(8,128)(2,1)S(1)}, bf16[2,128,2176]{2,1,0:T(8,128)(2,1)S(1)}, u32[]{:S(2)}, u32[]{:S(2)}) collective-permute-start(bf16[2,128,2176]{2,1,0:T(8,128)(2,1)S(1)} %pad_maximum_fusion.7), channel_id=1, source_target_pairs={{0,8},{4,12},{8,0},{12,4},{1,9},{5,13},{9,1},{13,5},{2,10},{6,14},... | collective-permute-start | bytes 3342344 | tf_op jit(solution)/shard_map/ppermute | solution.py:21
  317.5 26.5 %collective-permute-start.53 = (bf16[2,128,2176]{2,1,0:T(8,128)(2,1)}, bf16[2,128,2176]{2,1,0:T(8,128)(2,1)S(1)}, u32[]{:S(2)}, u32[]{:S(2)}) collective-permute-start(bf16[2,128,2176]{2,1,0:T(8,128)(2,1)} %pad_maximum_fusion.6), channel_id=1, source_target_pairs={{0,4},{4,0},{8,12},{12,8},{1,5},{5,1},{9,13},{13,9},{2,6},{6,2},{1... | collective-permute-start | bytes 3342344 | tf_op jit(solution)/shard_map/ppermute | solution.py:21
  350.8 36.7 %collective-permute-start.51 = (bf16[4,256,2048]{2,1,0:T(8,128)(2,1)}, bf16[4,256,2048]{2,1,0:T(8,128)(2,1)}, u32[]{:S(2)}, u32[]{:S(2)}) collective-permute-start(bf16[4,256,2048]{2,1,0:T(8,128)(2,1)} %get-tuple-element.82), channel_id=1, source_target_pairs={{0,16},{16,0},{1,17},{17,1},{2,18},{18,2},{3,19},{19,3},{4,20},{20... | collective-permute-start | bytes 12582920 | tf_op jit(solution)/shard_map/ppermute | solution.py:21
  371.7 22.4 %collective-permute-start.58 = (bf16[256,640]{1,0:T(8,128)(2,1)S(1)}, bf16[256,640]{1,0:T(8,128)(2,1)S(1)}, u32[]{:S(2)}, u32[]{:S(2)}) collective-permute-start(bf16[256,640]{1,0:T(8,128)(2,1)S(1)} %get-tuple-element.301), channel_id=1, source_target_pairs={{0,2},{1,3},{2,0},{3,1},{4,6},{5,7},{6,4},{7,5},{8,10},{9,11},{10,... | collective-permute-start | bytes 983048 | tf_op jit(solution)/shard_map/ppermute | solution.py:21
  396.2 33.8 %collective-permute-start.66 = (bf16[256,512]{1,0:T(8,128)(2,1)}, bf16[256,512]{1,0:T(8,128)(2,1)}, u32[]{:S(2)}, u32[]{:S(2)}) collective-permute-start(bf16[256,512]{1,0:T(8,128)(2,1)} %get-tuple-element.210.refs_5_), channel_id=1, source_target_pairs={{0,3},{1,2},{2,1},{3,0},{4,7},{5,6},{6,5},{7,4},{8,11},{9,10},{10,... | collective-permute-start | bytes 786440 | tf_op jit(solution)/shard_map/ppermute | solution.py:21
  397.3 39.6 %collective-permute-start.64 = (bf16[256,512]{1,0:T(8,128)(2,1)}, bf16[256,512]{1,0:T(8,128)(2,1)}, u32[]{:S(2)}, u32[]{:S(2)}) collective-permute-start(bf16[256,512]{1,0:T(8,128)(2,1)} %get-tuple-element.210.refs_5_), channel_id=1, source_target_pairs={{0,1},{1,0},{2,3},{3,2},{4,5},{5,4},{6,7},{7,6},{8,9},{9,8},{10,11... | collective-permute-start | bytes 786440 | tf_op jit(solution)/shard_map/ppermute | solution.py:21
  401.0 35.9 %collective-permute-start.65 = (bf16[256,512]{1,0:T(8,128)(2,1)}, bf16[256,512]{1,0:T(8,128)(2,1)}, u32[]{:S(2)}, u32[]{:S(2)}) collective-permute-start(bf16[256,512]{1,0:T(8,128)(2,1)} %get-tuple-element.210.refs_5_), channel_id=1, source_target_pairs={{0,2},{1,3},{2,0},{3,1},{4,6},{5,7},{6,4},{7,5},{8,10},{9,11},{10,... | collective-permute-start | bytes 786440 | tf_op jit(solution)/shard_map/ppermute | solution.py:21
  405.8 24.2 %collective-permute-start.61 = (bf16[2,128,2048]{2,1,0:T(8,128)(2,1)S(1)}, bf16[2,128,2048]{2,1,0:T(8,128)(2,1)S(1)}, u32[]{:S(2)}, u32[]{:S(2)}) collective-permute-start(bf16[2,128,2048]{2,1,0:T(8,128)(2,1)S(1)} %pad_maximum_fusion.12), channel_id=1, source_target_pairs={{0,8},{4,12},{8,0},{12,4},{1,9},{5,13},{9,1},{13,5},{2,10},{6,14},... | collective-permute-start | bytes 3145736 | tf_op jit(solution)/shard_map/ppermute | solution.py:21
  407.1 22.9 %collective-permute-start.60 = (bf16[2,128,2048]{2,1,0:T(8,128)(2,1)S(1)}, bf16[2,128,2048]{2,1,0:T(8,128)(2,1)S(1)}, u32[]{:S(2)}, u32[]{:S(2)}) collective-permute-start(bf16[2,128,2048]{2,1,0:T(8,128)(2,1)S(1)} %pad_maximum_fusion.11), channel_id=1, source_target_pairs={{0,4},{4,0},{8,12},{12,8},{1,5},{5,1},{9,13},{13,9},{2,6},{6,2},{1... | collective-permute-start | bytes 3145736 | tf_op jit(solution)/shard_map/ppermute | solution.py:21
  (179 other events, 1430.8 us)

commit v2 on v1

--- a/solution.py
+++ b/solution.py
@@ -328,7 +328,7 @@
 
         return carry
 
-    lax.fori_loop(0, group_count, body, 0)
+    lax.fori_loop(0, group_count, body, 0, unroll=2)
     for turn in range(group_count - 2, group_count):
         copy(turn, 0).wait()
 
@@ -378,7 +378,7 @@
 
     @pl.when(step == 0)
     def _():
-        lax.fori_loop(0, group_count, pick, 0)
+        lax.fori_loop(0, group_count, pick, 0, unroll=2)
 
     one = step // pieces
     start = pl.multiple_of(lax.rem(step, pieces) * piece_rows, piece_rows)
@@ -551,7 +551,7 @@
         + [pl.BlockSpec(memory_space=pl.ANY)] * len(earlier),
         out_specs=[pl.BlockSpec((1, tall, size), lambda i: (i // pieces, 0, 0))] * count,
         compiler_params=compiler_params(),
-        cost_estimate=cost(80),
+        cost_estimate=cost(20),
     )(left, right, *earlier)
 
 
@@ -1194,7 +1194,7 @@
             total = total + wide(swap(low(parts[rel]), TS, rel))
         return total
 
-    attn_part = scatter_dot(group, attended_low, out_blocks, out_cut, F32)
+    attn_part = scatter_dot(group, attended_low, out_blocks, out_cut, BF16)
     attn_share = tensor_sum(tensor_parts(attn_part))
     residual_share = wide(tokens.reshape(rows, quarter)) + attn_share
     grad_blocks = gather_context(hold(grad_output, *key_value[1:]), residual_share)

time: 599 us -> 595 us (level)
    unnamed x233 -> x229, local copies, waits for them, and re-layouts: 41.9 us -> 41.5 us
where the time goes in v2:
time: 595 us; the launch traced here: 585 us
  Pallas kernels  169 us (28%)
  waiting for transfers between devices  156 us (26%)
  starting transfers between devices  104 us (17%)
  local copies, waits for them, and re-layouts  85.8 us (14%)
  other arithmetic  66.1 us (11%)
    ppermute x97, waiting for transfers between devices, swap(): return lax.ppermute(value, axis, [(i, i ^ rel) for i in range(count)])  156 us
    ppermute x97, starting transfers between devices, swap(): return lax.ppermute(value, axis, [(i, i ^ rel) for i in range(count)])  104 us
    pallas_call x1, Pallas kernels, experts(): pl.pallas_call(functools.partial(experts_kernel, group_count, pad, pieces...  46.8 us
    unnamed x229, local copies, waits for them, and re-layouts  41.5 us
    pallas_call x2, Pallas kernels, weight_grad(): pl.pallas_call(functools.partial(weight_grad_kernel, pieces, len(earlier)...  35.1 us
    pallas_call x1, Pallas kernels, expert_out(): pl.pallas_call(functools.partial(expert_out_kernel, pad, pieces, len(earl...  16.4 us
  transfers between devices with their start and end apart: 97, of which 40 were waited for; matrix products, arithmetic and copies ran while one was open for 17% of the time, Pallas kernels for 26%

profile of v2, /device:TPU:8, one launch (start us, length us, event | category | flops | bytes accessed | tf_op | source)
XLA Modules:
  0.0 584.6 jit_solution(8049798083199169893)
XLA Ops:
  57.4 7.5 %collective-permute-done.15 = bf16[2,256,512]{2,1,0:T(8,128)(2,1)S(1)} collective-permute-done((bf16[2,256,512]{2,1,0:T(8,128)(2,1)}, bf16[2,256,512]{2,1,0:T(8,128)(2,1)S(1)}, u32[]{:S(2)}, u32[]{:S(2)}) %collective-permute-start.15) | collective-permute-done | bytes 524320 | tf_op jit(solution)/shard_map/ppermute | solution.py:21
  77.3 7.7 %shard_map.275 = (bf16[256,2048]{1,0:T(8,128)(2,1)}, f32[256,1536]{1,0:T(8,128)}, f32[3,256,1]{2,1,0:T(8,128)}, f32[256,1]{1,0:T(8,128)}, f32[2,2048]{1,0:T(2,128)}, /*index=5*/f32[1,1024]{1,0:T(1,128)}) custom-call(s32[1]{0:T(128)} %bitcast.1.index_ref.refs_0_, bf16[256,2048]{1,0:T(8,128)(2,1)} %pad_maximum_fusion.8.hidden_ref, ...), custom_call_target="tpu_custom_call" | custom-call | flops 12000000000 | tf_op jit(solution)/shard_map/pallas_call | solution.py:737
  107.0 5.1 convert_reduce_fusion
  127.8 6.0 %shard_map.284 = (bf16[256,512]{1,0:T(8,128)(2,1)}, f32[4,256,1]{2,1,0:T(8,128)}) custom-call(bf16[256,512]{1,0:T(8,128)(2,1)} %shard_map.279.query_ref, f32[256,1024]{1,0:T(8,128)} %add_select_fusion.bias_ref, bf16[256,1024]{1,0:T(8,128)(2,1)} %shard_map.283.refs_0_, bf16[256,1024]{1,0:T(8,128)(2,1)} %copy-done.53, bf16[256,1024]{1,0:T(8,128)(2,1)} %copy-done.54, ...), custom_call_target="tpu_custom_call" | custom-call | flops 12000000000 | tf_op jit(solution)/shard_map/pallas_call | solution.py:616
  143.1 7.3 %collective-permute-done.25 = bf16[256,512]{1,0:T(8,128)(2,1)S(1)} collective-permute-done((bf16[256,512]{1,0:T(8,128)(2,1)}, bf16[256,512]{1,0:T(8,128)(2,1)S(1)}, u32[]{:S(2)}, u32[]{:S(2)}) %collective-permute-start.25) | collective-permute-done | bytes 262176 | tf_op jit(solution)/shard_map/ppermute | solution.py:21
  150.4 8.4 %collective-permute-done.26 = bf16[256,512]{1,0:T(8,128)(2,1)S(1)} collective-permute-done((bf16[256,512]{1,0:T(8,128)(2,1)S(1)}, bf16[256,512]{1,0:T(8,128)(2,1)S(1)}, u32[]{:S(2)}, u32[]{:S(2)}) %collective-permute-start.26) | collective-permute-done | bytes 262176 | tf_op jit(solution)/shard_map/ppermute | solution.py:21
  181.0 6.8 %collective-permute-done.34.refs_0_ = bf16[256,512]{1,0:T(8,128)(2,1)S(1)} collective-permute-done((bf16[256,512]{1,0:T(8,128)(2,1)}, bf16[256,512]{1,0:T(8,128)(2,1)S(1)}, u32[]{:S(2)}, u32[]{:S(2)}) %collective-permute-start.34) | collective-permute-done | bytes 262176 | tf_op jit(solution)/shard_map/ppermute | solution.py:21
  207.3 9.9 %shard_map.292.refs_1_ = bf16[8,8,48,2048]{3,2,1,0:T(8,128)(2,1)} custom-call(s32[8,8,256]{2,1,0:T(8,128)} %fusion.86.refs_1_.slots_ref, bf16[256,2048]{1,0:T(8,128)(2,1)} %shard_map.286.refs_0_, bf16[256,2048]{1,0:T(8,128)(2,1)} %shard_map.287.refs_1_, bf16[256,2048]{1,0:T(8,128)(2,1)} %shard_map.288.refs_2_, bf16[256,2048]{1,0:T(8,128)(2,1)} %shard_map.291.refs_3_, ...), custom_call_target="tpu_custom_call" | custom-call | flops 12000000000 | tf_op jit(solution)/shard_map/pallas_call | solution.py:290
  217.2 9.8 %collective-permute-done.36.refs_0_ = bf16[256,2176]{1,0:T(8,128)(2,1)S(1)} collective-permute-done((bf16[256,2176]{1,0:T(8,128)(2,1)}, bf16[256,2176]{1,0:T(8,128)(2,1)S(1)}, u32[]{:S(2)}, u32[]{:S(2)}) %collective-permute-start.36) | collective-permute-done | bytes 1114144 | tf_op jit(solution)/shard_map/ppermute | solution.py:21
  238.8 5.7 collective-permute-done.38
  258.7 46.8 %shard_map.295 = (bf16[8,384,2048]{2,1,0:T(8,128)(2,1)}, bf16[8,384,256]{2,1,0:T(8,128)(2,1)}, bf16[8,384,512]{2,1,0:T(8,128)(2,1)}, bf16[256,2176]{1,0:T(8,128)...) custom-call(s32[1]{0:T(128)} %bitcast.30.first_ref, ...), custom_call_target="tpu_custom_call" | custom-call | flops 99999997952 | tf_op jit(solution)/shard_map/pallas_call | solution.py:436
  317.4 16.4 %shard_map.304 = (bf16[256,2048]{1,0:T(8,128)(2,1)}, bf16[256,2048]{1,0:T(8,128)(2,1)}, bf16[256,2048]{1,0:T(8,128)(2,1)}, bf16[256,2048]{1,0:T(8,128)(2,1)}, bf16[4,256,2048]{2,1,0:T(8,128)(2,1)}) custom-call(s32[8,8,256]{2,1,0:T(8,128)} %fusion.86.refs_1_.slots_ref, bf16[8,384,256]{2,1,0:T(8,128)(2,1)} %get-tuple-element.75.act_ref.left_ref, ...), custom_call_target="tpu_custom_call" | custom-call | flops 40000000000 | tf_op jit(solution)/shard_map/pallas_call | solution.py:483
  333.7 6.7 %collective-permute-done.54.refs_1_.refs_0_ = bf16[2,128,2176]{2,1,0:T(8,128)(2,1)S(1)} collective-permute-done((bf16[2,128,2176]{2,1,0:T(8,128)(2,1)S(1)}, bf16[2,128,2176]{2,1,0:T(8,128)(2,1)S(1)}, u32[]{:S(2)}, u32[]{:S(2)}) %collective-permute-start.54) | collective-permute-done | bytes 1114144 | tf_op jit(solution)/shard_map/ppermute | solution.py:21
  349.7 10.6 %collective-permute-done.56 = bf16[128,2176]{1,0:T(8,128)(2,1)S(1)} collective-permute-done((bf16[128,2176]{1,0:T(8,128)(2,1)S(1)}, bf16[128,2176]{1,0:T(8,128)(2,1)S(1)}, u32[]{:S(2)}, u32[]{:S(2)}) %collective-permute-start.56) | collective-permute-done | bytes 557088 | tf_op jit(solution)/shard_map/ppermute | solution.py:21
  370.3 15.2 %shard_map.307.refs_1_ = f32[8,256,2048]{2,1,0:T(8,128)} custom-call(bf16[8,384,256]{2,1,0:T(8,128)(2,1)} %get-tuple-element.75.act_ref.left_ref, bf16[8,384,2048]{2,1,0:T(8,128)(2,1)} %bitcast.323, f32[256,2176]{1,0:T(8,128)} %pad_maximum_fusion.1.outs_0_), custom_call_target="tpu_custom_call" | custom-call | flops 20000000000 | tf_op jit(solution)/shard_map/pallas_call | solution.py:546
  405.0 19.9 %shard_map.310 = (f32[8,2048,256]{2,1,0:T(8,128)}, f32[8,2048,256]{2,1,0:T(8,128)}) custom-call(bf16[8,384,2048]{2,1,0:T(8,128)(2,1)} %get-tuple-element.90.left_ref, bf16[8,384,512]{2,1,0:T(8,128)(2,1)} %get-tuple-element.91.right_ref, f32[256,512]{1,0:T(8,128)} %get-tuple-element.211.refs_1_.outs_0_), custom_call_target="tpu_custom_call" | custom-call | flops 20000000000 | tf_op jit(solution)/shard_map/pallas_call | solution.py:546
  433.9 5.7 shard_map.314
  439.6 7.7 %shard_map.315 = (f32[256,512]{1,0:T(8,128)}, bf16[256,1024]{1,0:T(8,128)(2,1)}, bf16[256,1024]{1,0:T(8,128)(2,1)}, bf16[256,1024]{1,0:T(8,128)(2,1)}, bf16[256,1024]{1,0:T(8,128)(2,1)}) custom-call(bf16[256,512]{1,0:T(8,128)(2,1)} %shard_map.279.query_ref, bf16[256,512]{1,0:T(8,128)(2,1)} %get-tuple-element.96.grad_ref, ...), custom_call_target="tpu_custom_call" | custom-call | flops 12000000000 | tf_op jit(solution)/shard_map/pallas_call | solution.py:657
  458.2 6.1 %collective-permute-done.68.refs_1_.refs_0_ = bf16[2,128,1024]{2,1,0:T(8,128)(2,1)S(1)} collective-permute-done((bf16[2,128,1024]{2,1,0:T(8,128)(2,1)}, bf16[2,128,1024]{2,1,0:T(8,128)(2,1)S(1)}, u32[]{:S(2)}, u32[]{:S(2)}) %collective-permute-start.68) | collective-permute-done | bytes 524320 | tf_op jit(solution)/shard_map/ppermute | solution.py:21
  475.5 6.8 %collective-permute-done.69 = bf16[128,1024]{1,0:T(8,128)(2,1)} collective-permute-done((bf16[128,1024]{1,0:T(8,128)(2,1)}, bf16[128,1024]{1,0:T(8,128)(2,1)}, u32[]{:S(2)}, u32[]{:S(2)}) %collective-permute-start.69) | collective-permute-done | bytes 262176 | tf_op jit(solution)/shard_map/ppermute | solution.py:21
  488.0 5.0 shard_map.319
  505.4 6.7 %shard_map.324 = (bf16[256,1536]{1,0:T(8,128)(2,1)}, bf16[256,2048]{1,0:T(8,128)(2,1)}) custom-call(s32[1]{0:T(128)} %bitcast.1.index_ref.refs_0_, f32[256,512]{1,0:T(8,128)} %get-tuple-element.103.refs_1_, f32[256,512]{1,0:T(8,128)} %get-tuple-element.104.refs_2_, bf16[256,512]{1,0:T(8,128)(2,1)} %get-tuple-element.105.refs_3_, ...), custom_call_target="tpu_custom_call" | custom-call | flops 12000000000 | tf_op jit(solution)/shard_map/pallas_call | solution.py:878
  565.0 10.8 %collective-permute-done.86 = bf16[256,512]{1,0:T(8,128)(2,1)S(1)} collective-permute-done((bf16[256,512]{1,0:T(8,128)(2,1)}, bf16[256,512]{1,0:T(8,128)(2,1)S(1)}, u32[]{:S(2)}, u32[]{:S(2)}) %collective-permute-start.86) | collective-permute-done | bytes 262176 | tf_op jit(solution)/shard_map/ppermute | solution.py:21
  578.1 6.3 %shard_map.330 = (f32[256,512]{1,0:T(8,128)}, f32[256,512]{1,0:T(8,128)}, f32[256,512]{1,0:T(8,128)}) custom-call(bf16[2,256,768]{2,1,0:T(8,128)(2,1)} %shard_map.329.refs_0_, bf16[2,256,768]{2,1,0:T(8,128)(2,1)} %collective-permute-done.45.refs_4_.refs_1_, bf16[2,256,768]{2,1,0:T(8,128)(2,1)} %collective-permute-done.46.refs_5_.refs_2_, ...), custom_call_target="tpu_custom_call" | custom-call | flops 8000000000 | tf_op jit(solution)/shard_map/pallas_call | solution.py:1070
  (642 shorter events, 336.6 us)
Async XLA Ops:
  8.8 22.7 %collective-permute-start.1 = (bf16[256,512]{1,0:T(8,128)(2,1)}, bf16[256,512]{1,0:T(8,128)(2,1)S(1)}, u32[]{:S(2)}, u32[]{:S(2)}) collective-permute-start(bf16[256,512]{1,0:T(8,128)(2,1)} %shard_map.272), channel_id=1, source_target_pairs={{0,2},{1,3},{2,0},{3,1},{4,6},{5,7},{6,4},{7,5},{8,10},{9,11},{10,... | collective-permute-start | bytes 786440 | tf_op jit(solution)/shard_map/ppermute | solution.py:21
  11.3 33.6 %collective-permute-start.4 = (bf16[256,1664]{1,0:T(8,128)(2,1)S(1)}, bf16[256,1664]{1,0:T(8,128)(2,1)}, u32[]{:S(2)}, u32[]{:S(2)}) collective-permute-start(bf16[256,1664]{1,0:T(8,128)(2,1)S(1)} %copy-done.36), channel_id=1, source_target_pairs={{0,8},{4,12},{8,0},{12,4},{1,9},{5,13},{9,1},{13,5},{2,10},{6,14},... | collective-permute-start | bytes 2555912 | tf_op jit(solution)/shard_map/ppermute | solution.py:21
  12.8 33.9 %collective-permute-start.3 = (bf16[256,1664]{1,0:T(8,128)(2,1)S(1)}, bf16[256,1664]{1,0:T(8,128)(2,1)S(1)}, u32[]{:S(2)}, u32[]{:S(2)}) collective-permute-start(bf16[256,1664]{1,0:T(8,128)(2,1)S(1)} %copy-done.36), channel_id=1, source_target_pairs={{0,4},{4,0},{8,12},{12,8},{1,5},{5,1},{9,13},{13,9},{2,6},{6,2},{1... | collective-permute-start | bytes 2555912 | tf_op jit(solution)/shard_map/ppermute | solution.py:21
  27.7 25.8 %collective-permute-start.7 = (bf16[256,1664]{1,0:T(8,128)(2,1)S(1)}, bf16[256,1664]{1,0:T(8,128)(2,1)}, u32[]{:S(2)}, u32[]{:S(2)}) collective-permute-start(bf16[256,1664]{1,0:T(8,128)(2,1)S(1)} %copy-done.36), channel_id=1, source_target_pairs={{0,16},{16,0},{1,17},{17,1},{2,18},{18,2},{3,19},{19,3},{4,20},{20... | collective-permute-start | bytes 2555912 | tf_op jit(solution)/shard_map/ppermute | solution.py:21
  41.4 23.4 %collective-permute-start.15 = (bf16[2,256,512]{2,1,0:T(8,128)(2,1)}, bf16[2,256,512]{2,1,0:T(8,128)(2,1)S(1)}, u32[]{:S(2)}, u32[]{:S(2)}) collective-permute-start(bf16[2,256,512]{2,1,0:T(8,128)(2,1)} %pad_maximum_fusion.27), channel_id=1, source_target_pairs={{0,2},{1,3},{2,0},{3,1},{4,6},{5,7},{6,4},{7,5},{8,10},{9,11},{10,... | collective-permute-start | bytes 1572872 | tf_op jit(solution)/shard_map/ppermute | solution.py:21
  46.8 28.6 %collective-permute-start.9 = (bf16[256,1664]{1,0:T(8,128)(2,1)}, bf16[256,1664]{1,0:T(8,128)(2,1)}, u32[]{:S(2)}, u32[]{:S(2)}) collective-permute-start(bf16[256,1664]{1,0:T(8,128)(2,1)} %shard_map.274.refs_2_.refs_10_.refs_9_), channel_id=1, source_target_pairs={{0,16},{16,0},{1,17},{17,1},{2,18},{18,2},{3,19},{19,3},{4,20},{20... | collective-permute-start | bytes 2555912 | tf_op jit(solution)/shard_map/ppermute | solution.py:21
  49.5 24.9 %collective-permute-start.8 = (bf16[256,1664]{1,0:T(8,128)(2,1)}, bf16[256,1664]{1,0:T(8,128)(2,1)}, u32[]{:S(2)}, u32[]{:S(2)}) collective-permute-start(bf16[256,1664]{1,0:T(8,128)(2,1)} %shard_map.273.refs_1_.refs_9_.refs_8_), channel_id=1, source_target_pairs={{0,16},{16,0},{1,17},{17,1},{2,18},{18,2},{3,19},{19,3},{4,20},{20... | collective-permute-start | bytes 2555912 | tf_op jit(solution)/shard_map/ppermute | solution.py:21
  71.8 22.1 %collective-permute-start.16 = (bf16[256,640]{1,0:T(8,128)(2,1)}, bf16[256,640]{1,0:T(8,128)(2,1)S(1)}, u32[]{:S(2)}, u32[]{:S(2)}) collective-permute-start(bf16[256,640]{1,0:T(8,128)(2,1)} %shard_map.280.refs_0_.refs_4_.refs_9_.refs_17_), channel_id=1, source_target_pairs={{0,4},{4,0},{8,12},{12,8},{1,5},{5,1},{9,13},{13,9},{2,6},{6,2},{1... | collective-permute-start | bytes 983048 | tf_op jit(solution)/shard_map/ppermute | solution.py:21
  126.0 41.9 %collective-permute-start.29 = (bf16[256,2048]{1,0:T(8,128)(2,1)}, bf16[256,2048]{1,0:T(8,128)(2,1)S(1)}, u32[]{:S(2)}, u32[]{:S(2)}) collective-permute-start(bf16[256,2048]{1,0:T(8,128)(2,1)} %shard_map.286.refs_0_), channel_id=1, source_target_pairs={{0,8},{4,12},{8,0},{12,4},{1,9},{5,13},{9,1},{13,5},{2,10},{6,14},... | collective-permute-start | bytes 3145736 | tf_op jit(solution)/shard_map/ppermute | solution.py:21
  127.5 37.8 %collective-permute-start.28 = (bf16[256,2048]{1,0:T(8,128)(2,1)}, bf16[256,2048]{1,0:T(8,128)(2,1)S(1)}, u32[]{:S(2)}, u32[]{:S(2)}) collective-permute-start(bf16[256,2048]{1,0:T(8,128)(2,1)} %shard_map.286.refs_0_), channel_id=1, source_target_pairs={{0,4},{4,0},{8,12},{12,8},{1,5},{5,1},{9,13},{13,9},{2,6},{6,2},{1... | collective-permute-start | bytes 3145736 | tf_op jit(solution)/shard_map/ppermute | solution.py:21
  199.8 27.2 %collective-permute-start.36 = (bf16[256,2176]{1,0:T(8,128)(2,1)}, bf16[256,2176]{1,0:T(8,128)(2,1)S(1)}, u32[]{:S(2)}, u32[]{:S(2)}) collective-permute-start(bf16[256,2176]{1,0:T(8,128)(2,1)} %get-tuple-element.74.refs_1_.refs_0_.refs_8_), channel_id=1, source_target_pairs={{0,4},{4,0},{8,12},{12,8},{1,5},{5,1},{9,13},{13,9},{2,6},{6,2},{1... | collective-permute-start | bytes 3342344 | tf_op jit(solution)/shard_map/ppermute | solution.py:21
  200.8 33.5 %collective-permute-start.37 = (bf16[256,2176]{1,0:T(8,128)(2,1)}, bf16[256,2176]{1,0:T(8,128)(2,1)S(1)}, u32[]{:S(2)}, u32[]{:S(2)}) collective-permute-start(bf16[256,2176]{1,0:T(8,128)(2,1)} %get-tuple-element.74.refs_1_.refs_0_.refs_8_), channel_id=1, source_target_pairs={{0,8},{4,12},{8,0},{12,4},{1,9},{5,13},{9,1},{13,5},{2,10},{6,14},... | collective-permute-start | bytes 3342344 | tf_op jit(solution)/shard_map/ppermute | solution.py:21
  255.2 50.3 %collective-permute-start.47 = (bf16[2,256,768]{2,1,0:T(8,128)(2,1)}, bf16[2,256,768]{2,1,0:T(8,128)(2,1)S(1)}, u32[]{:S(2)}, u32[]{:S(2)}) collective-permute-start(bf16[2,256,768]{2,1,0:T(8,128)(2,1)} %shard_map.299), channel_id=1, source_target_pairs={{0,12},{4,8},{8,4},{12,0},{1,13},{5,9},{9,5},{13,1},{2,14},{6,10},... | collective-permute-start | bytes 2359304 | tf_op jit(solution)/shard_map/ppermute | solution.py:21
  256.8 48.7 %collective-permute-start.46 = (bf16[2,256,768]{2,1,0:T(8,128)(2,1)}, bf16[2,256,768]{2,1,0:T(8,128)(2,1)}, u32[]{:S(2)}, u32[]{:S(2)}) collective-permute-start(bf16[2,256,768]{2,1,0:T(8,128)(2,1)} %shard_map.298), channel_id=1, source_target_pairs={{0,8},{4,12},{8,0},{12,4},{1,9},{5,13},{9,1},{13,5},{2,10},{6,14},... | collective-permute-start | bytes 2359304 | tf_op jit(solution)/shard_map/ppermute | solution.py:21
  258.4 47.2 %collective-permute-start.45 = (bf16[2,256,768]{2,1,0:T(8,128)(2,1)}, bf16[2,256,768]{2,1,0:T(8,128)(2,1)}, u32[]{:S(2)}, u32[]{:S(2)}) collective-permute-start(bf16[2,256,768]{2,1,0:T(8,128)(2,1)} %shard_map.297), channel_id=1, source_target_pairs={{0,4},{4,0},{8,12},{12,8},{1,5},{5,1},{9,13},{13,9},{2,6},{6,2},{1... | collective-permute-start | bytes 2359304 | tf_op jit(solution)/shard_map/ppermute | solution.py:21
  307.7 42.0 %collective-permute-start.52 = (bf16[256,2176]{1,0:T(8,128)(2,1)S(1)}, bf16[256,2176]{1,0:T(8,128)(2,1)}, u32[]{:S(2)}, u32[]{:S(2)}) collective-permute-start(bf16[256,2176]{1,0:T(8,128)(2,1)S(1)} %copy-done), channel_id=1, source_target_pairs={{0,16},{16,0},{1,17},{17,1},{2,18},{18,2},{3,19},{19,3},{4,20},{20... | collective-permute-start | bytes 3342344 | tf_op jit(solution)/shard_map/ppermute | solution.py:21
  313.7 26.7 %collective-permute-start.54 = (bf16[2,128,2176]{2,1,0:T(8,128)(2,1)S(1)}, bf16[2,128,2176]{2,1,0:T(8,128)(2,1)S(1)}, u32[]{:S(2)}, u32[]{:S(2)}) collective-permute-start(bf16[2,128,2176]{2,1,0:T(8,128)(2,1)S(1)} %pad_maximum_fusion.7), channel_id=1, source_target_pairs={{0,8},{4,12},{8,0},{12,4},{1,9},{5,13},{9,1},{13,5},{2,10},{6,14},... | collective-permute-start | bytes 3342344 | tf_op jit(solution)/shard_map/ppermute | solution.py:21
  316.3 26.5 %collective-permute-start.53 = (bf16[2,128,2176]{2,1,0:T(8,128)(2,1)}, bf16[2,128,2176]{2,1,0:T(8,128)(2,1)S(1)}, u32[]{:S(2)}, u32[]{:S(2)}) collective-permute-start(bf16[2,128,2176]{2,1,0:T(8,128)(2,1)} %pad_maximum_fusion.6), channel_id=1, source_target_pairs={{0,4},{4,0},{8,12},{12,8},{1,5},{5,1},{9,13},{13,9},{2,6},{6,2},{1... | collective-permute-start | bytes 3342344 | tf_op jit(solution)/shard_map/ppermute | solution.py:21
  349.7 35.9 %collective-permute-start.51 = (bf16[4,256,2048]{2,1,0:T(8,128)(2,1)}, bf16[4,256,2048]{2,1,0:T(8,128)(2,1)}, u32[]{:S(2)}, u32[]{:S(2)}) collective-permute-start(bf16[4,256,2048]{2,1,0:T(8,128)(2,1)} %get-tuple-element.82), channel_id=1, source_target_pairs={{0,16},{16,0},{1,17},{17,1},{2,18},{18,2},{3,19},{19,3},{4,20},{20... | collective-permute-start | bytes 12582920 | tf_op jit(solution)/shard_map/ppermute | solution.py:21
  392.8 34.1 %collective-permute-start.66 = (bf16[256,512]{1,0:T(8,128)(2,1)}, bf16[256,512]{1,0:T(8,128)(2,1)}, u32[]{:S(2)}, u32[]{:S(2)}) collective-permute-start(bf16[256,512]{1,0:T(8,128)(2,1)} %get-tuple-element.210.refs_5_), channel_id=1, source_target_pairs={{0,3},{1,2},{2,1},{3,0},{4,7},{5,6},{6,5},{7,4},{8,11},{9,10},{10,... | collective-permute-start | bytes 786440 | tf_op jit(solution)/shard_map/ppermute | solution.py:21
  394.3 39.6 %collective-permute-start.64 = (bf16[256,512]{1,0:T(8,128)(2,1)}, bf16[256,512]{1,0:T(8,128)(2,1)}, u32[]{:S(2)}, u32[]{:S(2)}) collective-permute-start(bf16[256,512]{1,0:T(8,128)(2,1)} %get-tuple-element.210.refs_5_), channel_id=1, source_target_pairs={{0,1},{1,0},{2,3},{3,2},{4,5},{5,4},{6,7},{7,6},{8,9},{9,8},{10,11... | collective-permute-start | bytes 786440 | tf_op jit(solution)/shard_map/ppermute | solution.py:21
  397.6 36.3 %collective-permute-start.65 = (bf16[256,512]{1,0:T(8,128)(2,1)}, bf16[256,512]{1,0:T(8,128)(2,1)}, u32[]{:S(2)}, u32[]{:S(2)}) collective-permute-start(bf16[256,512]{1,0:T(8,128)(2,1)} %get-tuple-element.210.refs_5_), channel_id=1, source_target_pairs={{0,2},{1,3},{2,0},{3,1},{4,6},{5,7},{6,4},{7,5},{8,10},{9,11},{10,... | collective-permute-start | bytes 786440 | tf_op jit(solution)/shard_map/ppermute | solution.py:21
  402.9 24.0 %collective-permute-start.61 = (bf16[2,128,2048]{2,1,0:T(8,128)(2,1)S(1)}, bf16[2,128,2048]{2,1,0:T(8,128)(2,1)S(1)}, u32[]{:S(2)}, u32[]{:S(2)}) collective-permute-start(bf16[2,128,2048]{2,1,0:T(8,128)(2,1)S(1)} %pad_maximum_fusion.12), channel_id=1, source_target_pairs={{0,8},{4,12},{8,0},{12,4},{1,9},{5,13},{9,1},{13,5},{2,10},{6,14},... | collective-permute-start | bytes 3145736 | tf_op jit(solution)/shard_map/ppermute | solution.py:21
  404.0 22.8 %collective-permute-start.60 = (bf16[2,128,2048]{2,1,0:T(8,128)(2,1)S(1)}, bf16[2,128,2048]{2,1,0:T(8,128)(2,1)S(1)}, u32[]{:S(2)}, u32[]{:S(2)}) collective-permute-start(bf16[2,128,2048]{2,1,0:T(8,128)(2,1)S(1)} %pad_maximum_fusion.11), channel_id=1, source_target_pairs={{0,4},{4,0},{8,12},{12,8},{1,5},{5,1},{9,13},{13,9},{2,6},{6,2},{1... | collective-permute-start | bytes 3145736 | tf_op jit(solution)/shard_map/ppermute | solution.py:21
  (177 other events, 1410.3 us)
